TPU v7x, 128 devices: a whole 4x4x4 slice. The times are simulated.
128 devices in a mesh: row: 4 (over z_hi, core), col: 32 (over x, y, z_lo).
Axes of the slice: x: 4, y: 4, z: 4 (z_hi: 2, z_lo: 2; z = z_hi * 2 + z_lo), core: 2. Of those that a mesh axis runs over, the one named last changes fastest.
Arguments:
- packed_input_rows: bfloat16 [4096, 8192], P('col', 'row'), may hold values from -6 to 6
- frozen_weight: bfloat16 [8192, 28672], P('row', 'col'), may hold values from -0.0625 to 0.0625
- down_adapters: float32 [16, 16, 8192], P(None, None, 'row'), may hold values from -6 to 6
- up_adapters: float32 [16, 16, 28672], P(None, None, 'col'), may hold values from -6 to 6
- trial_learning_rates: float32 [16], replicated, may hold values from 0.03 to 0.3
- row_trial_index: int32 [4096], replicated, may hold values from 0 to 15, never falling along the last dimension, each value on 1 to 512 neighbouring positions
- output_gradient: bfloat16 [4096, 28672], P('row', 'col'), may hold values from -6 to 6
- keeper_slot: int32 [16], replicated, may hold values from 0 to 15, as said below
Outputs:
- projected: bfloat16 [4096, 28672], P('row', 'col')
- new_down: float32 [16, 16, 8192], P(None, None, 'row')
- new_up: float32 [16, 16, 28672], P(None, None, 'col')
Inputs may be any that keep to these rules, and one draw needn't show every extreme that they name: `row_trial_index`: never falls along the rows; every trial owns 1 to 512 rows, one trial exactly 512. `keeper_slot`: exactly 8 slots hold their own index, slot 0 and slot 15 among them; each other slot holds the index of a different one of those.
All inputs are finite; a program needn't handle non-finite values.
Results may differ from a plain program's by a relative error of at most 0.0054.
Values may be sent and summed in bfloat16 or wider, within the bound.
A program may use at most 192 MiB of HBM per device.

v0:
```python
import jax
import jax.numpy as jnp
from jax import lax
from jax.sharding import PartitionSpec as P

D = 8192
ADAPTER_RANK = 16


def per_device(
    packed_input_rows,
    frozen_weight,
    down_adapters,
    up_adapters,
    trial_learning_rates,
    row_trial_index,
    output_gradient,
    keeper_slot,
):
    adapter_scale = 2.0 / ADAPTER_RANK
    inv_width = D ** (-0.5)
    trials = down_adapters.shape[0]
    ranks = down_adapters.shape[1]
    width_in = down_adapters.shape[2]
    width_out = up_adapters.shape[2]
    flat_width = trials * ranks
    contract_last = (((1,), (1,)), ((), ()))
    reduce_leading = (((0,), (0,)), ((), ()))
    down_low = down_adapters.astype(jnp.bfloat16)
    up_flat = up_adapters.astype(jnp.bfloat16).reshape(flat_width, width_out)
    gathered = lax.all_gather(packed_input_rows, "col", axis=0, tiled=True)
    all_rows = gathered.shape[0]
    block_rows = output_gradient.shape[0]
    seg_most = 2 * all_rows // trials
    trial_labels = jnp.arange(trials, dtype=jnp.int32)
    block_start = lax.axis_index("row") * block_rows
    block_ids = lax.dynamic_slice_in_dim(row_trial_index, block_start, block_rows)
    member_block = (block_ids[:, None] == trial_labels[None, :]).astype(jnp.float32)

    def window_start(trial):
        first = jnp.sum((row_trial_index < trial).astype(jnp.int32))
        return jnp.minimum(first, all_rows - seg_most)

    def hidden_trial(trial, totals):
        start = window_start(trial)
        window = lax.dynamic_slice_in_dim(gathered, start, seg_most, 0)
        window_ids = lax.dynamic_slice_in_dim(row_trial_index, start, seg_most)
        adapter = lax.dynamic_index_in_dim(down_low, trial, 0, keepdims=False)
        product = lax.dot_general(
            window, adapter, contract_last, preferred_element_type=jnp.float32
        )
        product = jnp.where((window_ids == trial)[:, None], product, 0.0)
        current = lax.dynamic_slice_in_dim(totals, start, seg_most, 0)
        return lax.dynamic_update_slice_in_dim(totals, current + product, start, 0)

    hidden_part = lax.fori_loop(0, trials, hidden_trial, jnp.zeros((all_rows, ranks), jnp.float32))
    hidden = lax.psum_scatter(hidden_part, "row", scatter_dimension=0, tiled=True) * inv_width
    hidden_low = hidden.astype(jnp.bfloat16)
    hidden_full = (member_block.astype(jnp.bfloat16)[:, :, None] * hidden_low[:, None, :]).reshape(
        block_rows, flat_width
    )
    frozen_term = lax.psum_scatter(
        jnp.dot(gathered, frozen_weight, preferred_element_type=jnp.float32),
        "row",
        scatter_dimension=0,
        tiled=True,
    )
    rank_hidden = jnp.dot(hidden_full, up_flat, preferred_element_type=jnp.float32)
    projected = (frozen_term + adapter_scale * rank_hidden).astype(jnp.bfloat16)
    gradient_full = lax.dot_general(
        output_gradient, up_flat, contract_last, preferred_element_type=jnp.float32
    )
    grad_block = jnp.sum(
        gradient_full.reshape(gradient_full.shape[0], trials, ranks) * member_block[:, :, None],
        axis=1,
    )
    gradient_spread = lax.dynamic_update_slice_in_dim(
        jnp.zeros((all_rows, ranks), jnp.float32), grad_block, block_start, 0
    )
    gradient_rows = lax.psum(gradient_spread, ("row", "col")) * adapter_scale
    grad_low = gradient_rows.astype(jnp.bfloat16)

    def down_trial(trial, totals):
        start = window_start(trial)
        window = lax.dynamic_slice_in_dim(gathered, start, seg_most, 0)
        window_ids = lax.dynamic_slice_in_dim(row_trial_index, start, seg_most)
        grads = lax.dynamic_slice_in_dim(grad_low, start, seg_most, 0)
        grads = jnp.where((window_ids == trial)[:, None], grads, jnp.zeros_like(grads))
        product = lax.dot_general(grads, window, reduce_leading, preferred_element_type=jnp.float32)
        return lax.dynamic_update_index_in_dim(totals, product, trial, 0)

    down_grad = (
        lax.fori_loop(0, trials, down_trial, jnp.zeros((trials, ranks, width_in), jnp.float32))
        * inv_width
    )
    adapter_term = lax.dot_general(
        hidden_full, output_gradient, reduce_leading, preferred_element_type=jnp.float32
    )
    up_gradient = lax.psum(adapter_term, "row") * adapter_scale
    rates = trial_learning_rates[:, None, None]
    moved_down = down_adapters - rates * down_grad
    moved_up = up_adapters - rates * up_gradient.reshape(trials, ranks, width_out)
    picked_trial = (keeper_slot[:, None] == trial_labels[None, :]).astype(jnp.float32)
    new_down = jnp.einsum("st,tkd->skd", picked_trial, moved_down, precision=lax.Precision.HIGHEST)
    new_up = jnp.einsum("st,tkf->skf", picked_trial, moved_up, precision=lax.Precision.HIGHEST)
    return (projected, new_down, new_up)


def solution(mesh):
    in_specs = (
        P("col", "row"),
        P("row", "col"),
        P(None, None, "row"),
        P(None, None, "col"),
        P(),
        P(),
        P("row", "col"),
        P(),
    )
    out_specs = (P("row", "col"), P(None, None, "row"), P(None, None, "col"))
    return jax.shard_map(
        per_device, mesh=mesh, in_specs=in_specs, out_specs=out_specs, check_vma=False
    )
```

profile of v0, /device:TPU:4, one launch (start us, length us, event | category | flops | bytes accessed | tf_op | source)
XLA Modules:
  0.0 733.5 jit_solution(16828712719490615760)
XLA Ops:
  12.9 371.5 %all-reduce.3.cloned.1.call-done = f32[4096,16]{0,1:T(8,128)} async-done(((f32[4096,16]{0,1:T(8,128)}), f32[4096,16]{0,1:T(8,128)}) %all-reduce.3.cloned.1.call-update) | async-done | bytes 262160 | tf_op jit(solution)/shard_map/psum | solution.py:80
  385.5 67.7 %while.27 = (s32[]{:T(128)}, f32[16,16,2048]{2,1,0:T(8,128)}, s32[4096]{0:T(1024)S(1)}, bf16[4096,16]{0,1:T(8,128)(2,1)S(1)}, bf16[4096,2048]{1,0:T(8,128)(2,1)}...) while((s32[]{:T(128)}, f32[16,16,2048]{2,1,0:T(8,128)}, s32[4096]{0:T(1024)S(1)}, ...), condition=%wide.region_9.10_spmd, body=%wide.region_7.9_spmd.sunk | while | flops 33575428 | bytes 2265755 | solution.py:93
  386.8 2.9 fusion.59
  391.1 2.9 fusion.59
  395.3 2.9 fusion.59
  399.5 2.9 fusion.59
  403.8 2.9 fusion.59
  408.0 2.9 fusion.59
  412.2 2.9 fusion.59
  416.5 2.9 fusion.59
  420.7 2.9 fusion.59
  424.9 2.9 fusion.59
  429.2 2.9 fusion.59
  433.4 2.9 fusion.59
  437.6 2.9 fusion.59
  441.9 2.9 fusion.59
  446.1 2.8 fusion.59
  450.3 2.8 fusion.59
  453.2 4.9 multiply_subtract_fusion
  458.1 66.8 %while.26 = (s32[]{:T(128)}, f32[4096,16]{0,1:T(8,128)S(1)}, s32[4096]{0:T(1024)S(1)}, bf16[4096,2048]{1,0:T(8,128)(2,1)}, bf16[16,16,2048]{2,1,0:T(8,128)(2,1)S...) while((s32[]{:T(128)}, f32[4096,16]{0,1:T(8,128)S(1)}, s32[4096]{0:T(1024)S(1)}, ...), condition=%wide.region_3.4_spmd, body=%wide.region_1.3_spmd.sunk | while | flops 33583620 | bytes 2314911 | solution.py:56
  467.8 2.3 fusion.56
  472.0 2.3 fusion.56
  476.2 2.3 fusion.56
  480.4 2.3 fusion.56
  488.9 2.3 fusion.56
  525.6 27.4 %reduce-scatter.5.cloned.1.call-done = f32[1024,16]{0,1:T(8,128)} async-done(((f32[4096,16]{0,1:T(8,128)}), f32[1024,16]{0,1:T(8,128)}) %reduce-scatter.5.cloned.1.call-update) | async-done | bytes 65552 | tf_op jit(solution)/shard_map/reduce_scatter | solution.py:57
  555.8 23.2 %fusion.42 = f32[4096,896]{1,0:T(8,128)} fusion(bf16[4096,2048]{1,0:T(8,128)(2,1)} %get-tuple-element.346, bf16[2048,896]{1,0:T(8,128)(2,1)} %param.13), kind=kOutput, calls=%fused_computation.48 | convolution fusion | flops 15032385536 | bytes 35127296 | tf_op jit(solution)/shard_map/dot_general | solution.py:63
  579.6 3.9 fusion.21
  583.5 2.5 copy.18
  586.1 14.0 %all-reduce.5.cloned.1.call-done = f32[256,896]{1,0:T(8,128)} async-done(((f32[256,896]{1,0:T(8,128)}), f32[256,896]{1,0:T(8,128)}) %all-reduce.5.cloned.1.call-update) | async-done | bytes 917520 | tf_op jit(solution)/shard_map/psum | solution.py:99
  603.5 118.9 %reduce-scatter.3.cloned.1.call-done = f32[1024,896]{1,0:T(8,128)} async-done(((f32[4096,896]{1,0:T(8,128)}), f32[1024,896]{1,0:T(8,128)}) %reduce-scatter.3.cloned.1.call-update) | async-done | bytes 3670032 | tf_op jit(solution)/shard_map/reduce_scatter | solution.py:62
  722.3 4.0 fusion.20
  (132 shorter events, 69.5 us)
Async XLA Ops:
  8.0 1.5 copy-start
  8.0 376.4 %all-reduce.3.cloned.1.call-start = ((), (), s32[]{:S(2)}) async-start(), calls=%async_computation.5 | async-start | bytes 524288 | tf_op jit(solution)/shard_map/psum | solution.py:80
  9.5 3.4 copy-start.6
  9.5 375.9 %copy-start.1 = (s32[4096]{0:T(1024)S(1)}, s32[4096]{0:T(1024)}, u32[]{:S(2)}) copy-start(s32[4096]{0:T(1024)} %param.17) | copy-start | bytes 49156
  11.5 0.7 copy-start.3
  12.3 373.2 %all-gather.2.cloned.1.call-start = ((), (), s32[]{:S(2)}) async-start(), calls=%async_computation.2 | async-start | bytes 17301504 | tf_op jit(solution)/shard_map/all_gather | solution.py:31
  12.8 540.2 %reduce-scatter.5.cloned.1.call-start = ((), (), s32[]{:S(2)}) async-start(), calls=%async_computation.4 | async-start | bytes 327680 | tf_op jit(solution)/shard_map/reduce_scatter | solution.py:57
  524.8 0.7 copy-start.2
  525.6 74.5 %all-reduce.5.cloned.1.call-start = ((), (), s32[]{:S(2)}) async-start(), calls=%async_computation.6 | async-start | bytes 1835008 | tf_op jit(solution)/shard_map/psum | solution.py:99
  555.6 166.8 %reduce-scatter.3.cloned.1.call-start = ((), (), s32[]{:S(2)}) async-start(), calls=%async_computation.3 | async-start | bytes 18350080 | tf_op jit(solution)/shard_map/reduce_scatter | solution.py:62
  579.0 0.7 copy-start.5
  583.5 17.8 %copy-start.4 = (f32[16,16,896]{2,1,0:T(8,128)S(1)}, f32[16,16,896]{2,1,0:T(8,128)}, u32[]{:S(2)}) copy-start(f32[16,16,896]{2,1,0:T(8,128)} %param.15) | copy-start | bytes 2752516
Sparse Core Ops, SparseCore 0:
  14.2 370.2 all-reduce.2
  525.7 27.2 reduce-scatter.4
  556.3 43.7 all-reduce.4
  602.8 119.4 reduce-scatter.2
Sparse Core Ops, SparseCore 1:
  14.4 364.3 all-gather.1
where the time goes:
time: 736 us; the launch traced here: 733 us
  waiting for transfers between devices  532 us (72%)
  matrix products  117 us (16%)
  other arithmetic  31.1 us (4%)
  loops' own time  21.5 us (3%)
  local copies, waits for them, and re-layouts  15.7 us (2%)
  between operations  15.4 us (2%)
    psum x1, waiting for transfers between devices, per_device(): gradient_rows = lax.psum(gradient_spread, ('row', 'col')) * adapter_scale  372 us
    reduce_scatter x1, waiting for transfers between devices, per_device(): lax.psum_scatter(jnp.dot(gathered, frozen_weight, preferred_element_type=...  119 us
    dot_general x16, matrix products, down_trial(): lax.dot_general(grads, window, reduce_leading, preferred_element_type=jnp...  45.7 us
    dot_general x16, matrix products, hidden_trial(): lax.dot_general(window, adapter, contract_last, preferred_element_type=jn...  36 us
    reduce_scatter x1, waiting for transfers between devices, per_device(): lax.psum_scatter(hidden_part, 'row', scatter_dimension=0, tiled=True)  27.4 us
    dot_general x1, matrix products, per_device(): jnp.dot(gathered, frozen_weight, preferred_element_type=jnp.float32)  23.2 us
    reduce_sum x32, other arithmetic, window_start(): first = jnp.sum((row_trial_index < trial).astype(jnp.int32))  20.3 us
  transfers between devices with their start and end apart: 5, of which 4 were waited for; matrix products, arithmetic and copies ran while one was open for 5% of the time, Pallas kernels for 0%

commit v1 on v0

v1 whole, which is shorter than its diff:
```python
import functools

import jax
import jax.numpy as jnp
from jax import lax
from jax.experimental import pallas as pl
from jax.experimental.pallas import tpu as pltpu
from jax.sharding import PartitionSpec as P

MESH = pl.DeviceIdType.MESH
D = 8192
RANK = 16
TRIALS = 16
FLAT = RANK * TRIALS
SHARD = 128
PIECE = 64
HALF = 32
SCALE = 2.0 / RANK
INV_WIDTH = D ** (-0.5)

STEPS = (
    (("F", 0),),
    (("L", 0, 0),),
    (("L", 1, 0),),
    (("RF", 0), ("RL", 0, 0)),
    (("F", 1),),
    (("L", 0, 1),),
    (("L", 3, 0),),
    (("L", 2, 0),),
    (("RF", 1), ("RL", 0, 1)),
    (("RL", 1, 0), ("RL", 3, 0)),
    (("L", 1, 1),),
    (("L", 3, 1),),
    (("L", 2, 1),),
    (("RL", 1, 1), ("RL", 3, 1)),
    (("RL", 2, 0), ("RL", 2, 1)),
)
ITEMS = tuple(item for step in STEPS for item in step)
Z_GROUP = 3
GROUPS = len(STEPS) + 1


def offsets(kind, first, last, zz):
    return (first, last, zz, 0) if kind == 0 else (last, first, zz, 1)


def landed(axis, item):
    name, zz = item[0], item[-1]
    kind = axis if name in ("F", "RF") else 1 - axis
    if name == "F":
        return [offsets(kind, 3, 0, zz), offsets(kind, 1, 0, zz)]
    if name == "RF":
        return [offsets(kind, 2, 0, zz)]
    if name == "L":
        return [offsets(kind, item[1], 3, zz), offsets(kind, item[1], 1, zz)]
    return [offsets(kind, item[1], 2, zz)]


def group_pieces():
    groups = []
    for step in STEPS:
        groups.append([piece for axis in (0, 1) for item in step for piece in landed(axis, item)])
    groups.insert(Z_GROUP, [(0, 0, 0, 0), (0, 0, 1, 0), (0, 0, 0, 1), (0, 0, 1, 1)])
    return groups


CODES = [[dx + 4 * dy + 16 * dz + 32 * kind for dx, dy, dz, kind in group] for group in group_pieces()]


def select(index, values):
    out = jnp.int32(values[0])
    for at in range(1, len(values)):
        out = jnp.where(index == at, jnp.int32(values[at]), out)
    return out


def gather_kernel(
    x_ref, w_ref, bounds_ref, grad_ref, hid_ref, up_ref, proj_ref, down_ref,
    xg, w_v, keep, stage, recv_core, total, z_stage, recv_z,
    local_sem, send_sem, recv_sem, z_send, z_recv, core_send, core_recv, far_send, far_recv,
):
    row = lax.axis_index("row")
    col = lax.axis_index("col")
    z_hi, core = row // 2, row % 2
    x, y, z_lo = col // 8, (col // 2) % 4, col % 2

    def base(piece):
        dx, dy, dz, kind = piece
        return ((x + dx) % 4 * 8 + (y + dy) % 4 * 2 + (z_lo + dz) % 2) * SHARD + kind * PIECE

    def neighbour(axis, way):
        if axis == 0:
            return (row, (x + way) % 4 * 8 + y * 2 + z_lo)
        return (row, x * 8 + (y + way) % 4 * 2 + z_lo)

    z_mate = (row, x * 8 + y * 2 + 1 - z_lo)
    core_mate = (z_hi * 2 + 1 - core, col)
    far_mate = ((1 - z_hi) * 2 + core, col)

    own = pltpu.make_async_copy(
        x_ref, xg.at[pl.ds(pl.multiple_of(col * SHARD, SHARD), SHARD)], local_sem.at[0]
    )
    own.start()
    weight = pltpu.make_async_copy(w_ref, w_v, local_sem.at[1])
    weight.start()

    barrier = pltpu.get_barrier_semaphore()
    mates = [neighbour(0, 1), neighbour(0, 3), neighbour(1, 1), neighbour(1, 3), z_mate, core_mate, far_mate]
    for mate in mates:
        pl.semaphore_signal(barrier, inc=1, device_id=mate, device_id_type=MESH)
    pl.semaphore_wait(barrier, len(mates))
    own.wait()

    def remote(start, rows, ssem, rsem, mate):
        spot = xg.at[pl.ds(pl.multiple_of(start, HALF), rows)]
        return pltpu.make_async_remote_copy(
            src_ref=spot, dst_ref=spot, send_sem=ssem, recv_sem=rsem, device_id=mate, device_id_type=MESH
        )

    def sending(axis, way, item):
        name, zz = item[0], item[-1]
        kind = axis if name in ("F", "RF") else 1 - axis
        back = 3 if way == 0 else 1
        if name == "F":
            start, rows = base(offsets(kind, 0, 0, zz)), PIECE
        elif name == "RF":
            start, rows = base(offsets(kind, back, 0, zz)) + way * HALF, HALF
        elif name == "L":
            start, rows = base(offsets(kind, item[1], 0, zz)), PIECE
        else:
            start, rows = base(offsets(kind, item[1], back, zz)) + way * HALF, HALF
        at = ITEMS.index(item)
        return remote(
            start, rows, send_sem.at[axis, way, at], recv_sem.at[axis, way, at],
            neighbour(axis, 1 if way == 0 else 3),
        )

    def receiving(axis, way, item):
        pieces = landed(axis, item)
        if len(pieces) == 2:
            start, rows = base(pieces[way]), PIECE
        else:
            start, rows = base(pieces[0]) + way * HALF, HALF
        at = ITEMS.index(item)
        return remote(
            start, rows, send_sem.at[axis, way, at], recv_sem.at[axis, way, at],
            neighbour(axis, 1 if way == 0 else 3),
        )

    def every(step, action):
        for item in STEPS[step]:
            for axis in (0, 1):
                for way in (0, 1):
                    action(axis, way, item)

    def send(step):
        every(step, lambda *what: sending(*what).start())

    def arrive(step):
        every(step, lambda *what: receiving(*what).wait_recv())

    def z_copy(kind, dz):
        return remote(base((0, 0, dz, kind)), PIECE, z_send.at[kind], z_recv.at[kind], z_mate)

    send(0)
    for kind in (0, 1):
        z_copy(kind, 0).start()
    send(1)
    weight.wait()
    down_ref[...] = jnp.zeros_like(down_ref)
    spread = (
        lax.broadcasted_iota(jnp.int32, (RANK, FLAT), 1) % RANK
        == lax.broadcasted_iota(jnp.int32, (RANK, FLAT), 0)
    ).astype(jnp.bfloat16)

    def expand(low, starts, rows):
        values = jnp.dot(low, spread, preferred_element_type=jnp.float32)
        parts = []
        for at, start in enumerate(starts):
            where = start + lax.broadcasted_iota(jnp.int32, (rows, FLAT), 0)
            inside = (where >= bounds_ref[0:1, :]) & (where < bounds_ref[1:2, :])
            parts.append(jnp.where(inside, values[at * rows:(at + 1) * rows], 0.0).astype(jnp.bfloat16))
        return jnp.concatenate(parts, axis=0)

    def decode(code):
        dx, dy, dz, kind = code % 4, code // 4 % 4, code // 16 % 2, code // 32
        return (x + dx) % 4, base((dx, dy, dz, kind))

    def core_copy(group, pair):
        return pltpu.make_async_remote_copy(
            src_ref=stage.at[group, pair], dst_ref=recv_core.at[group, pair],
            send_sem=core_send.at[group, pair], recv_sem=core_recv.at[group, pair],
            device_id=core_mate, device_id_type=MESH,
        )

    def far_copy(number):
        spot = pl.ds(pl.multiple_of(number * PIECE, PIECE), PIECE)
        return pltpu.make_async_remote_copy(
            src_ref=z_stage.at[spot], dst_ref=recv_z.at[spot],
            send_sem=far_send.at[number], recv_sem=far_recv.at[number],
            device_id=far_mate, device_id_type=MESH,
        )

    def group_codes(group):
        return [decode(select(group, [codes[slot] for codes in CODES])) for slot in range(4)]

    def body(group, carry):
        for step in range(len(STEPS)):
            @pl.when(group == (step if step < Z_GROUP else step + 1))
            def _():
                arrive(step)
                if step == Z_GROUP - 1:
                    for kind in (0, 1):
                        z_copy(kind, 1).wait_recv()
                if step + 2 < len(STEPS):
                    send(step + 2)

        @pl.when(group < GROUPS)
        def _():
            places = group_codes(group)
            starts = [pl.multiple_of(start, PIECE) for _, start in places]
            rows = jnp.concatenate([xg[pl.ds(start, PIECE), :] for start in starts], axis=0)
            product = jnp.dot(rows, w_v[...], preferred_element_type=jnp.float32)
            keep[group % 2] = product
            for pair in (0, 1):
                stage[group, pair] = product[pair * 2 * PIECE:(pair + 1) * 2 * PIECE].astype(jnp.bfloat16)

                @pl.when(places[2 * pair][0] % 2 != core)
                def _():
                    core_copy(group, pair).start()

            low = jnp.concatenate([grad_ref[pl.ds(start, PIECE), :] for start in starts], axis=0)
            down_ref[...] += lax.dot_general(
                expand(low, starts, PIECE), rows, (((0,), (0,)), ((), ())), preferred_element_type=jnp.float32
            )

        @pl.when(group > 0)
        def _():
            past = group - 1
            places = group_codes(past)
            for pair in (0, 1):
                @pl.when(places[2 * pair][0] % 2 == core)
                def _():
                    core_copy(past, pair).wait_recv()
                    for half in (0, 1):
                        plane, start = places[2 * pair + half]
                        number = start % (8 * SHARD) // PIECE
                        spot = pl.ds(pl.multiple_of(number * PIECE, PIECE), PIECE)
                        rows = slice(half * PIECE, (half + 1) * PIECE)
                        summed = (
                            keep[past % 2, pl.ds((2 * pair + half) * PIECE, PIECE), :]
                            + recv_core[past, pair, rows, :].astype(jnp.float32)
                        )

                        @pl.when(plane // 2 == z_hi)
                        def _():
                            total[spot, :] = summed

                        @pl.when(plane // 2 != z_hi)
                        def _():
                            z_stage[spot, :] = summed.astype(jnp.bfloat16)
                            far_copy(number).start()

        return carry

    lax.fori_loop(0, GROUPS + 1, body, 0)

    def finish(number, carry):
        far_copy(number).wait_recv()
        start = pl.multiple_of(number * PIECE, PIECE)
        spot = pl.ds(start, PIECE)
        full = expand(hid_ref[spot, :], [row * 8 * SHARD + start], PIECE)
        adapter = jnp.dot(full, up_ref[...], preferred_element_type=jnp.float32)
        proj_ref[spot, :] = (
            total[spot, :] + recv_z[spot, :].astype(jnp.float32) + SCALE * adapter
        ).astype(jnp.bfloat16)
        return carry

    lax.fori_loop(0, 16, finish, 0)

    for step in range(len(STEPS)):
        every(step, lambda *what: sending(*what).wait_send())
    for kind in (0, 1):
        z_copy(kind, 0).wait_send()

    def drain(number, carry):
        far_copy(number).wait_send()
        return carry

    lax.fori_loop(0, 16, drain, 0)

    def drain_core(group, carry):
        places = group_codes(group)
        for pair in (0, 1):
            @pl.when(places[2 * pair][0] % 2 != core)
            def _():
                core_copy(group, pair).wait_send()

        return carry

    lax.fori_loop(0, GROUPS, drain_core, 0)


def per_device(
    packed_input_rows,
    frozen_weight,
    down_adapters,
    up_adapters,
    trial_learning_rates,
    row_trial_index,
    output_gradient,
    keeper_slot,
):
    width_in, width_out = frozen_weight.shape
    all_rows = row_trial_index.shape[0]
    block_rows = output_gradient.shape[0]
    contract_last = (((1,), (1,)), ((), ()))
    reduce_leading = (((0,), (0,)), ((), ()))
    row, col = lax.axis_index("row"), lax.axis_index("col")
    labels = jnp.arange(TRIALS, dtype=jnp.int32)
    down_flat = down_adapters.astype(jnp.bfloat16).reshape(FLAT, width_in)
    up_flat = up_adapters.astype(jnp.bfloat16).reshape(FLAT, width_out)
    ends = jnp.sum((row_trial_index[None, :] <= labels[:, None]).astype(jnp.int32), axis=1)
    starts = jnp.concatenate([jnp.zeros((1,), jnp.int32), ends[:-1]])
    bounds = jnp.repeat(jnp.stack([starts, ends]), RANK, axis=1)

    def member(start, rows):
        ids = lax.dynamic_slice_in_dim(row_trial_index, start, rows)
        return (ids[:, None] == labels[None, :]).astype(jnp.float32)

    def own_trial(full, start):
        rows = full.shape[0]
        return jnp.sum(full.reshape(rows, TRIALS, RANK) * member(start, rows)[:, :, None], axis=1)

    hidden_full = lax.dot_general(
        packed_input_rows, down_flat, contract_last, preferred_element_type=jnp.float32
    )
    hidden = lax.psum(own_trial(hidden_full, col * SHARD), "row") * INV_WIDTH
    hidden_low = lax.all_gather(hidden.astype(jnp.bfloat16), "col", axis=0, tiled=True)
    hidden_low = lax.dynamic_slice_in_dim(hidden_low, row * block_rows, block_rows)
    gradient_full = lax.dot_general(
        output_gradient, up_flat, contract_last, preferred_element_type=jnp.float32
    )
    gradient = lax.psum(own_trial(gradient_full, row * block_rows), "col") * SCALE
    grad_low = lax.all_gather(gradient.astype(jnp.bfloat16), "row", axis=0, tiled=True)
    hidden_wide = (
        member(row * block_rows, block_rows).astype(jnp.bfloat16)[:, :, None] * hidden_low[:, None, :]
    ).reshape(block_rows, FLAT)
    up_gradient = lax.psum(
        lax.dot_general(hidden_wide, output_gradient, reduce_leading, preferred_element_type=jnp.float32), "row"
    ) * SCALE

    vmem = pl.BlockSpec(memory_space=pltpu.VMEM)
    hbm = pl.BlockSpec(memory_space=pl.ANY)
    dma = pltpu.SemaphoreType.DMA
    projected, down_grad = pl.pallas_call(
        gather_kernel,
        name="gather_project",
        out_shape=(
            jax.ShapeDtypeStruct((block_rows, width_out), jnp.bfloat16),
            jax.ShapeDtypeStruct((FLAT, width_in), jnp.float32),
        ),
        in_specs=[hbm, hbm, vmem, vmem, vmem, vmem],
        out_specs=(vmem, vmem),
        scratch_shapes=[
            pltpu.VMEM((all_rows, width_in), jnp.bfloat16),
            pltpu.VMEM((width_in, width_out), jnp.bfloat16),
            pltpu.VMEM((2, 4 * PIECE, width_out), jnp.float32),
            pltpu.VMEM((GROUPS, 2, 2 * PIECE, width_out), jnp.bfloat16),
            pltpu.VMEM((GROUPS, 2, 2 * PIECE, width_out), jnp.bfloat16),
            pltpu.VMEM((block_rows, width_out), jnp.float32),
            pltpu.VMEM((block_rows, width_out), jnp.bfloat16),
            pltpu.VMEM((block_rows, width_out), jnp.bfloat16),
            dma((2,)),
            dma((2, 2, len(ITEMS))),
            dma((2, 2, len(ITEMS))),
            dma((2,)),
            dma((2,)),
            dma((GROUPS, 2)),
            dma((GROUPS, 2)),
            dma((16,)),
            dma((16,)),
        ],
        compiler_params=pltpu.CompilerParams(
            collective_id=0, has_side_effects=True, vmem_limit_bytes=60 << 20
        ),
        cost_estimate=pl.CostEstimate(flops=20 * 10**9, bytes_accessed=30 << 20, transcendentals=0),
    )(packed_input_rows, frozen_weight, bounds, grad_low, hidden_low, up_flat)

    rates = trial_learning_rates[:, None, None]
    moved_down = down_adapters - rates * (down_grad * INV_WIDTH).reshape(down_adapters.shape)
    moved_up = up_adapters - rates * up_gradient.reshape(up_adapters.shape)
    new_down = jnp.take(moved_down, keeper_slot, axis=0, mode="clip")
    new_up = jnp.take(moved_up, keeper_slot, axis=0, mode="clip")
    return (projected, new_down, new_up)


def solution(mesh):
    in_specs = (
        P("col", "row"),
        P("row", "col"),
        P(None, None, "row"),
        P(None, None, "col"),
        P(),
        P(),
        P("row", "col"),
        P(),
    )
    out_specs = (P("row", "col"), P(None, None, "row"), P(None, None, "col"))
    return jax.shard_map(
        per_device, mesh=mesh, in_specs=in_specs, out_specs=out_specs, check_vma=False
    )
```

time: 736 us -> 608 us (0.83)
  waiting for transfers between devices: 532 us -> 337 us
  Pallas kernels: 0 us -> 125 us
  matrix products: 117 us -> 4.58 us
  blocking collectives: 0 us -> 104 us
  other arithmetic: 31.1 us -> 8.05 us
  loops' own time: 21.5 us -> 0 us
    reduce_scatter x2 -> x0, waiting for transfers between devices: 146 us -> none  [the longest x1 119 us: per_device(): lax.psum_scatter(jnp.dot(gathered, frozen_weight, preferred_element_type=...]
    pallas_call x0 -> x1, Pallas kernels: none -> 125 us  [per_device(): pl.pallas_call(gather_kernel, name='gather_project', out_shape=(jax.Shape...]
    dot_general x37 -> x2, matrix products: 115 us -> 3.84 us  [the longest x1 2.21 us: per_device(): lax.dot_general(packed_input_rows, down_flat, contract_last, preferred_el...]
    all_gather x0 -> x2, blocking collectives: none -> 87 us  [the longest x1 74.9 us: per_device(): lax.all_gather(hidden.astype(jnp.bfloat16), 'col', axis=0, tiled=True)]
    psum x2, waiting for transfers between devices: 385 us -> 337 us  [the longest x1 287 us: per_device(): lax.psum(own_trial(gradient_full, row * block_rows), 'col') * SCALE]
    another operation x2 -> x0, loops' own time: 21.5 us -> none  [the longest x1 10.9 us: per_device(): lax.fori_loop(0, trials, hidden_trial, jnp.zeros((all_rows, ranks), jnp.f...]
    reduce_sum x32 -> x1, other arithmetic: 20.3 us -> 0.15 us  [per_device(): jnp.sum((row_trial_index[None, :] <= labels[:, None]).astype(jnp.int32),...]
    psum x0 -> x1, blocking collectives: none -> 17.4 us  [per_device(): hidden = lax.psum(own_trial(hidden_full, col * SHARD), 'row') * INV_WIDTH]
  transfers between devices with their start and end apart: 5 -> 2, of which waited for: 4 -> 2; matrix products, arithmetic and copies ran while one was open for 5% -> 0% of each run, Pallas kernels for 0% -> 0%
where the time goes in v1:
time: 608 us; the launch traced here: 604 us
  waiting for transfers between devices  337 us (55%)
  Pallas kernels  125 us (21%)
  blocking collectives  104 us (17%)
  between operations  14.2 us (2%)
  local copies, waits for them, and re-layouts  11.2 us (2%)
  other arithmetic  8.05 us (1%)
    psum x1, waiting for transfers between devices, per_device(): lax.psum(own_trial(gradient_full, row * block_rows), 'col') * SCALE  287 us
    pallas_call x1, Pallas kernels, per_device(): pl.pallas_call(gather_kernel, name='gather_project', out_shape=(jax.Shape...  125 us
    all_gather x1, blocking collectives, per_device(): lax.all_gather(hidden.astype(jnp.bfloat16), 'col', axis=0, tiled=True)  74.9 us
    psum x1, waiting for transfers between devices, per_device(): lax.psum(lax.dot_general(hidden_wide, output_gradient, reduce_leading, pr...  50.1 us
    psum x1, blocking collectives, per_device(): hidden = lax.psum(own_trial(hidden_full, col * SHARD), 'row') * INV_WIDTH  17.4 us
  transfers between devices with their start and end apart: 2, of which 2 were waited for; matrix products, arithmetic and copies ran while one was open for 0% of the time, Pallas kernels for 0%

profile of v1, /device:TPU:4, one launch (start us, length us, event | category | flops | bytes accessed | tf_op | source)
XLA Modules:
  0.0 604.2 jit_solution(5496669287836280402)
XLA Ops:
  7.2 0.0 copy-start
  7.2 0.0 all-reduce.5.cloned.1.call-start
  7.2 0.9 dynamic_slice.11
  8.1 2.2 fusion.8
  10.4 0.1 copy.17
  10.5 17.4 %psum.22 = f32[128,16]{1,0:T(8,128)S(1)} all-reduce(f32[128,16]{1,0:T(8,128)S(1)} %copy.17), channel_id=1, replica_groups=mesh['row'=4,'col'=32] {'row'}, use_global_device_ids=true, to_apply=%region_4.0 | all-reduce | flops 2048 | bytes 16384 | tf_op jit(solution)/shard_map/psum | solution.py:338
  27.9 74.9 %all_gather.7 = bf16[4096,16]{1,0:T(8,128)(2,1)S(1)} all-gather(bf16[128,16]{1,0:T(8,128)(2,1)S(1)} %multiply_convert_fusion.1), channel_id=1, replica_groups=mesh['row'=4,'col'=32] {'col'}, dimensions={0}, use_global_device_ids=true | all-gather | bytes 135168 | tf_op jit(solution)/shard_map/all_gather | solution.py:339
  102.7 0.1 copy.18
  102.9 0.1 broadcast_multiply_fusion.2
  102.9 1.6 fusion.14
  104.6 0.0 all-reduce.5.cloned.1.call-update
  104.6 0.0 all-reduce.3.cloned.1.call-start
  104.7 0.1 convert_reduce_fusion
  104.8 0.1 add_bitcast_fusion
  104.9 0.1 broadcast_in_dim.6
  105.0 0.7 reshape.94.bounds_ref
  105.6 50.1 %all-reduce.5.cloned.1.call-done = f32[256,896]{1,0:T(8,128)} async-done(((f32[256,896]{1,0:T(8,128)}), f32[256,896]{1,0:T(8,128)}) %all-reduce.5.cloned.1.call-update) | async-done | bytes 917520 | tf_op jit(solution)/shard_map/psum | solution.py:349
  155.8 1.2 broadcast_multiply_fusion.1
  157.0 1.7 multiply_subtract_fusion.1
  158.8 0.7 fusion.5
  159.5 1.0 copy.16
  160.5 0.0 all-reduce.3.cloned.1.call-update
  160.6 1.5 gather_fusion.1
  162.1 286.6 %all-reduce.3.cloned.1.call-done = f32[1024,16]{1,0:T(8,128)} async-done(((f32[1024,16]{1,0:T(8,128)}), f32[1024,16]{1,0:T(8,128)}) %all-reduce.3.cloned.1.call-update) | async-done | bytes 65552 | tf_op jit(solution)/shard_map/psum | solution.py:344
  448.7 1.1 multiply_convert_fusion
  449.8 12.1 %all_gather.6.grad_ref = bf16[4096,16]{1,0:T(8,128)(2,1)} all-gather(bf16[1024,16]{1,0:T(8,128)(2,1)S(1)} %multiply_convert_fusion), channel_id=1, replica_groups=mesh['row'=4,'col'=32] {'row'}, dimensions={0}, use_global_device_ids=true | all-gather | bytes 163840 | tf_op jit(solution)/shard_map/all_gather | solution.py:345
  461.9 125.0 %gather_project.1 = (bf16[1024,896]{1,0:T(8,128)(2,1)}, f32[256,2048]{1,0:T(8,128)}) custom-call(bf16[128,2048]{1,0:T(8,128)(2,1)} %x_ref.1, bf16[2048,896]{1,0:T(8,128)(2,1)} %w_ref.1, s32[2,256]{1,0:T(2,128)} %reshape.94.bounds_ref, bf16[4096,16]{1,0:T(8,128)(2,1)} %all_gather.6.grad_ref, bf16[1024,16]{1,0:T(8,128)(2,1)} %copy-done.2, ...), custom_call_target="tpu_custom_call" | custom-call | flops 20000000000 | bytes 31457280 | tf_op jit(solution)/shard_map/gather_project/pallas_call | solution.py:356
  586.9 1.9 broadcast_multiply_fusion
  588.9 0.3 copy-done.1
  589.1 1.8 multiply_subtract_fusion
  590.9 3.6 gather_fusion
  594.5 2.9 copy.22
  (20 shorter events, 0.1 us)
Async XLA Ops:
  7.2 95.8 %copy-start = (bf16[1024,896]{1,0:T(8,128)(2,1)S(1)}, bf16[1024,896]{1,0:T(8,128)(2,1)}, u32[]{:S(2)}) copy-start(bf16[1024,896]{1,0:T(8,128)(2,1)} %param.14) | copy-start | bytes 5505028
  7.2 148.6 %all-reduce.5.cloned.1.call-start = ((), (), s32[]{:S(2)}) async-start(), calls=%async_computation.1 | async-start | bytes 1835008 | tf_op jit(solution)/shard_map/psum | solution.py:349
  7.2 20.6 %dynamic-slice-start = ((s32[4096]{0:T(1024)}, s32[]{:T(128)}), s32[1024]{0:T(1024)S(1)}, s32[]{:S(2)}) async-start(s32[4096]{0:T(1024)} %param.13, s32[]{:T(128)} %select_n.8), calls=%async_computation.2 | async-start | bytes 8704 | tf_op jit(solution)/shard_map/dynamic_slice | solution.py:328
  102.7 1.9 copy-start.2
  102.9 1.7 copy-start.4
  104.6 52.4 %copy-start.5 = (f32[16]{0:T(128)S(1)}, f32[16]{0:T(128)}, u32[]{:S(2)}) copy-start(f32[16]{0:T(128)} %param.12) | copy-start | bytes 196
  104.6 344.1 %all-reduce.3.cloned.1.call-start = ((), (), s32[]{:S(2)}) async-start(), calls=%async_computation | async-start | bytes 1048576 | tf_op jit(solution)/shard_map/psum | solution.py:344
  158.8 0.8 copy-start.3
  158.8 1.8 copy-start.6
  586.9 2.2 copy-start.1
Sparse Core Ops, SparseCore 0:
  104.7 50.9 all-reduce.4
  160.7 288.0 all-reduce.2

commit v2 on v1

v2 whole, which is shorter than its diff:
```python
import jax
import jax.numpy as jnp
from jax import lax
from jax.experimental import pallas as pl
from jax.experimental.pallas import tpu as pltpu
from jax.sharding import PartitionSpec as P

MESH = pl.DeviceIdType.MESH
D = 8192
RANK = 16
TRIALS = 16
FLAT = RANK * TRIALS
SHARD = 128
PIECE = 64
HALF = 32
SCALE = 2.0 / RANK
INV_WIDTH = D ** (-0.5)

STEPS = (
    (("F", 0),),
    (("L", 0, 0),),
    (("L", 1, 0),),
    (("RF", 0), ("RL", 0, 0)),
    (("F", 1),),
    (("L", 0, 1),),
    (("L", 3, 0),),
    (("L", 2, 0),),
    (("RF", 1), ("RL", 0, 1)),
    (("RL", 1, 0), ("RL", 3, 0)),
    (("L", 1, 1),),
    (("L", 3, 1),),
    (("L", 2, 1),),
    (("RL", 1, 1), ("RL", 3, 1)),
    (("RL", 2, 0), ("RL", 2, 1)),
)
ITEMS = tuple(item for step in STEPS for item in step)
Z_GROUP = 3
GROUPS = len(STEPS) + 1


def offsets(kind, first, last, zz):
    return (first, last, zz, 0) if kind == 0 else (last, first, zz, 1)


def landed(axis, item):
    name, zz = item[0], item[-1]
    kind = axis if name in ("F", "RF") else 1 - axis
    if name == "F":
        return [offsets(kind, 3, 0, zz), offsets(kind, 1, 0, zz)]
    if name == "RF":
        return [offsets(kind, 2, 0, zz)]
    if name == "L":
        return [offsets(kind, item[1], 3, zz), offsets(kind, item[1], 1, zz)]
    return [offsets(kind, item[1], 2, zz)]


def group_pieces():
    groups = []
    for step in STEPS:
        groups.append([piece for axis in (0, 1) for item in step for piece in landed(axis, item)])
    groups.insert(Z_GROUP, [(0, 0, 0, 0), (0, 0, 1, 0), (0, 0, 0, 1), (0, 0, 1, 1)])
    return groups


CODES = [[dx + 4 * dy + 16 * dz + 32 * kind for dx, dy, dz, kind in group] for group in group_pieces()]


def pair_slots():
    seen, slots = [0, 0], []
    for group in group_pieces():
        slots.append([])
        for pair in (0, 1):
            odd = group[2 * pair][0] % 2
            slots[-1].append(seen[odd])
            seen[odd] += 1
    return slots


SLOTS = pair_slots()
PAIRS = 16
SMALL = (
    ["hid_core", "hid_far", "hid_z"] + [f"hid_y{k}" for k in (1, 2, 3)] + [f"hid_x{k}" for k in (1, 2, 3)]
    + [f"grad_x{k}" for k in (1, 2, 3)] + [f"grad_y{k}" for k in (1, 2, 3)] + ["grad_z"]
    + [f"low_x{k}" for k in (1, 2, 3)] + ["low_core", "low_far", "up_core", "up_far", "up_share"]
)
CATCH_UP = 6


def select(index, values):
    out = jnp.int32(values[0])
    for at in range(1, len(values)):
        out = jnp.where(index == at, jnp.int32(values[at]), out)
    return out


def whole_kernel(
    x_ref, w_ref, down_ref, up_ref, rate_ref, trial_ref, grad_ref, keeper_ref,
    proj_ref, new_down_ref, new_up_ref,
    xg, w_v, keep, stage, recv_core, total, z_stage, recv_z,
    down_v, down_low, up_v, up_low, grad_v, down_sum, grad_wide, hid_wide,
    hid_part, hid_core, hid_half, hid_far, hid_low,
    grad_part, grad_x, grad_y, grad_z, grad_low,
    up_part, up_core, up_half, up_far, up_sum,
    local_sem, send_sem, recv_sem, z_send, z_recv, core_send, core_recv, far_send, far_recv,
    small_send, small_recv,
):
    row = lax.axis_index("row")
    col = lax.axis_index("col")
    z_hi, core = row // 2, row % 2
    x, y, z_lo = col // 8, (col // 2) % 4, col % 2
    contract_last = (((1,), (1,)), ((), ()))
    contract_first = (((0,), (0,)), ((), ()))

    def base(piece):
        dx, dy, dz, kind = piece
        return ((x + dx) % 4 * 8 + (y + dy) % 4 * 2 + (z_lo + dz) % 2) * SHARD + kind * PIECE

    def neighbour(axis, way):
        if axis == 0:
            return (row, (x + way) % 4 * 8 + y * 2 + z_lo)
        return (row, x * 8 + (y + way) % 4 * 2 + z_lo)

    z_mate = (row, x * 8 + y * 2 + 1 - z_lo)
    core_mate = (z_hi * 2 + 1 - core, col)
    far_mate = ((1 - z_hi) * 2 + core, col)

    loads = [
        pltpu.make_async_copy(source, target, local_sem.at[at])
        for at, (source, target) in enumerate((
            (x_ref, xg.at[pl.ds(pl.multiple_of(col * SHARD, SHARD), SHARD)]),
            (down_ref, down_v), (up_ref, up_v), (grad_ref, grad_v), (w_ref, w_v),
        ))
    ]
    for load in loads:
        load.start()
    own, down_load, up_load, grad_load, weight_load = loads

    barrier = pltpu.get_barrier_semaphore()
    mates = [neighbour(axis, way) for axis in (0, 1) for way in (1, 2, 3)] + [z_mate, core_mate, far_mate]
    for mate in mates:
        pl.semaphore_signal(barrier, inc=1, device_id=mate, device_id_type=MESH)
    pl.semaphore_wait(barrier, len(mates))
    own.wait()

    def remote(start, rows, ssem, rsem, mate):
        spot = xg.at[pl.ds(pl.multiple_of(start, HALF), rows)]
        return pltpu.make_async_remote_copy(
            src_ref=spot, dst_ref=spot, send_sem=ssem, recv_sem=rsem, device_id=mate, device_id_type=MESH
        )

    def sending(axis, way, item):
        name, zz = item[0], item[-1]
        kind = axis if name in ("F", "RF") else 1 - axis
        back = 3 if way == 0 else 1
        if name == "F":
            start, rows = base(offsets(kind, 0, 0, zz)), PIECE
        elif name == "RF":
            start, rows = base(offsets(kind, back, 0, zz)) + way * HALF, HALF
        elif name == "L":
            start, rows = base(offsets(kind, item[1], 0, zz)), PIECE
        else:
            start, rows = base(offsets(kind, item[1], back, zz)) + way * HALF, HALF
        at = ITEMS.index(item)
        return remote(
            start, rows, send_sem.at[axis, way, at], recv_sem.at[axis, way, at],
            neighbour(axis, 1 if way == 0 else 3),
        )

    def receiving(axis, way, item):
        pieces = landed(axis, item)
        if len(pieces) == 2:
            start, rows = base(pieces[way]), PIECE
        else:
            start, rows = base(pieces[0]) + way * HALF, HALF
        at = ITEMS.index(item)
        return remote(
            start, rows, send_sem.at[axis, way, at], recv_sem.at[axis, way, at],
            neighbour(axis, 1 if way == 0 else 3),
        )

    def every(step, action):
        for item in STEPS[step]:
            for axis in (0, 1):
                for way in (0, 1):
                    action(axis, way, item)

    def send(step):
        every(step, lambda *what: sending(*what).start())

    def arrive(step):
        every(step, lambda *what: receiving(*what).wait_recv())

    def z_copy(kind, dz):
        return remote(base((0, 0, dz, kind)), PIECE, z_send.at[kind], z_recv.at[kind], z_mate)

    send(0)
    for kind in (0, 1):
        z_copy(kind, 0).start()
    send(1)

    def small(name, source, target, mate):
        at = SMALL.index(name)
        return pltpu.make_async_remote_copy(
            src_ref=source, dst_ref=target, send_sem=small_send.at[at], recv_sem=small_recv.at[at],
            device_id=mate, device_id_type=MESH,
        )

    half = pl.ds(core * (TRIALS // 2), TRIALS // 2)
    other_half = pl.ds((1 - core) * (TRIALS // 2), TRIALS // 2)
    sends = {
        "hid_core": lambda: small("hid_core", hid_part, hid_core, core_mate),
        "hid_far": lambda: small("hid_far", hid_half, hid_far, far_mate),
        "hid_z": lambda: small("hid_z", hid_low.at[col], hid_low.at[col], z_mate),
        "grad_z": lambda: small("grad_z", grad_z.at[z_lo], grad_z.at[z_lo], z_mate),
        "low_core": lambda: small(
            "low_core", grad_low.at[pl.ds(row * 4, 4)], grad_low.at[pl.ds(row * 4, 4)], core_mate),
        "low_far": lambda: small(
            "low_far", grad_low.at[pl.ds(z_hi * 8, 8)], grad_low.at[pl.ds(z_hi * 8, 8)], far_mate),
        "up_core": lambda: small("up_core", up_part.at[other_half], up_core, core_mate),
        "up_far": lambda: small("up_far", up_half, up_far, far_mate),
        "up_share": lambda: small("up_share", up_sum.at[half], up_sum.at[half], core_mate),
    }
    for way in (1, 2, 3):
        def along(way=way):
            to_x, to_y = neighbour(0, way), neighbour(1, way)
            block, plane = pl.ds(x * 8 + y * 2, 2), pl.ds(x * 8, 8)
            sends[f"hid_y{way}"] = lambda: small(f"hid_y{way}", hid_low.at[block], hid_low.at[block], to_y)
            sends[f"hid_x{way}"] = lambda: small(f"hid_x{way}", hid_low.at[plane], hid_low.at[plane], to_x)
            sends[f"grad_x{way}"] = lambda: small(
                f"grad_x{way}", grad_part.at[(x + way) % 4], grad_x.at[x], to_x)
            sends[f"grad_y{way}"] = lambda: small(f"grad_y{way}", grad_y.at[y], grad_y.at[y], to_y)
            own_chunk = row * 4 + x
            sends[f"low_x{way}"] = lambda: small(
                f"low_x{way}", grad_low.at[own_chunk], grad_low.at[own_chunk], to_x)
        along()

    def go(*names):
        for name in names:
            sends[name]().start()

    def come(*names):
        for name in names:
            sends[name]().wait_recv()

    def trio(name):
        return [f"{name}{way}" for way in (1, 2, 3)]

    def bounds(shape, axis):
        label = lax.broadcasted_iota(jnp.int32, shape, axis) // RANK
        low, high = jnp.zeros(shape, jnp.int32), jnp.zeros(shape, jnp.int32)
        first = jnp.zeros((1, 1), jnp.int32)
        for trial in range(TRIALS):
            count = jnp.sum((trial_ref[...] <= trial).astype(jnp.int32), keepdims=True)
            low = jnp.where(label == trial, first, low)
            high = jnp.where(label == trial, count, high)
            first = count
        return low, high

    lane_low, lane_high = bounds((1, FLAT), 1)
    side_low, side_high = bounds((FLAT, 1), 0)
    spread = (
        lax.broadcasted_iota(jnp.int32, (RANK, FLAT), 1) % RANK
        == lax.broadcasted_iota(jnp.int32, (RANK, FLAT), 0)
    ).astype(jnp.bfloat16)

    def pick_rank(full, start):
        rows = full.shape[1]
        where = start + lax.broadcasted_iota(jnp.int32, (FLAT, rows), 1)
        mine = jnp.where((where >= side_low) & (where < side_high), full, 0.0)
        return jnp.sum(mine.reshape(TRIALS, RANK, rows), axis=0)

    def widen(low, start):
        values = lax.dot_general(low, spread, contract_first, preferred_element_type=jnp.float32)
        where = start + lax.broadcasted_iota(jnp.int32, values.shape, 0)
        return jnp.where((where >= lane_low) & (where < lane_high), values, 0.0).astype(jnp.bfloat16)

    down_load.wait()

    def cast_down(trial, carry):
        down_low[pl.ds(pl.multiple_of(trial * RANK, RANK), RANK), :] = down_v[trial].astype(jnp.bfloat16)
        return carry

    lax.fori_loop(0, TRIALS, cast_down, 0)
    own_rows = xg[pl.ds(pl.multiple_of(col * SHARD, SHARD), SHARD), :]
    hid_part[...] = pick_rank(
        lax.dot_general(down_low[...], own_rows, contract_last, preferred_element_type=jnp.float32), col * SHARD
    )
    go("hid_core")

    up_load.wait()
    for trial in range(TRIALS):
        up_low[trial * RANK:(trial + 1) * RANK, :] = up_v[trial].astype(jnp.bfloat16)
    grad_load.wait()

    def gradient_chunk(chunk, carry):
        start = pl.multiple_of(chunk * 256, 256)
        full = lax.dot_general(
            up_low[...], grad_v[pl.ds(start, 256), :], contract_last, preferred_element_type=jnp.float32
        )
        grad_part[chunk] = pick_rank(full, row * 8 * SHARD + start)
        return carry

    lax.fori_loop(0, 4, gradient_chunk, 0)
    go(*trio("grad_x"))
    grad_x[x] = grad_part[x]
    down_sum[...] = jnp.zeros_like(down_sum)
    total[...] = jnp.zeros_like(total)
    weight_load.wait()

    def small_0():
        come("hid_core")
        hid_half[...] = hid_part[...] + hid_core[...]
        go("hid_far")
        come(*trio("grad_x"))
        grad_y[y] = (grad_x[0] + grad_x[1]) + (grad_x[2] + grad_x[3])
        go(*trio("grad_y"))

    def small_1():
        come("hid_far")
        hid_low[col] = ((hid_half[...] + hid_far[...]) * INV_WIDTH).astype(jnp.bfloat16)
        go("hid_z")
        come(*trio("grad_y"))
        grad_z[z_lo] = (grad_y[0] + grad_y[1]) + (grad_y[2] + grad_y[3])
        go("grad_z")

    def small_2():
        come("hid_z")
        go(*trio("hid_y"))
        come("grad_z")
        grad_low[row * 4 + x] = ((grad_z[0] + grad_z[1]) * SCALE).astype(jnp.bfloat16)
        go(*trio("low_x"))

    def small_3():
        come(*trio("hid_y"))

        @pl.when(x == row)
        def _():
            go(*trio("hid_x"))

        come(*trio("low_x"))
        go("low_core")

    def small_4():
        for way in (1, 2, 3):
            @pl.when((x - way + 4) % 4 == row)
            def _():
                sends[f"hid_x{way}"]().wait_recv()

        def wide(block, carry):
            start = pl.multiple_of(block * SHARD, SHARD)
            hid_wide[pl.ds(start, SHARD), :] = widen(hid_low[row * 8 + block], row * 8 * SHARD + start)
            return carry

        lax.fori_loop(0, 8, wide, 0)
        full = lax.dot_general(hid_wide[...], grad_v[...], contract_first, preferred_element_type=jnp.float32)
        up_part[...] = full.reshape(up_part.shape)
        go("up_core")
        come("low_core")
        go("low_far")

    def small_5():
        come("up_core")
        up_half[...] = up_part[half] + up_core[...]
        go("up_far")
        come("low_far")

        def wide(chunk, carry):
            start = pl.multiple_of(chunk * 256, 256)
            grad_wide[pl.ds(start, 256), :] = widen(grad_low[chunk], start)
            return carry

        lax.fori_loop(0, 16, wide, 0)

    def small_6():
        come("up_far")
        up_sum[half] = up_half[...] + up_far[...]
        go("up_share")

    def small_7():
        come("up_share")

        def moved(slot, carry):
            trial = keeper_ref[slot]
            new_up_ref[slot] = up_v[trial] - rate_ref[trial] * (up_sum[trial] * SCALE)
            return carry

        lax.fori_loop(0, TRIALS, moved, 0)

    def small_8():
        def adapter(block, carry):
            spot = pl.ds(pl.multiple_of(block * SHARD, SHARD), SHARD)
            total[spot, :] += SCALE * jnp.dot(
                hid_wide[spot, :], up_low[...], preferred_element_type=jnp.float32
            )
            return carry

        lax.fori_loop(0, 8, adapter, 0)

    smalls = [small_0, small_1, small_2, small_3, small_4, small_5, small_6, small_7, small_8]

    def decode(code):
        dx, dy, dz, kind = code % 4, code // 4 % 4, code // 16 % 2, code // 32
        return (x + dx) % 4, base((dx, dy, dz, kind))

    def core_copy(slot):
        return pltpu.make_async_remote_copy(
            src_ref=stage.at[slot], dst_ref=recv_core.at[slot],
            send_sem=core_send.at[slot], recv_sem=core_recv.at[slot],
            device_id=core_mate, device_id_type=MESH,
        )

    def far_copy(number):
        spot = pl.ds(pl.multiple_of(number * PIECE, PIECE), PIECE)
        return pltpu.make_async_remote_copy(
            src_ref=z_stage.at[spot], dst_ref=recv_z.at[spot],
            send_sem=far_send.at[number], recv_sem=far_recv.at[number],
            device_id=far_mate, device_id_type=MESH,
        )

    def group_places(group):
        return [decode(select(group, [codes[slot] for codes in CODES])) for slot in range(4)]

    def group_rows(places):
        starts = [pl.multiple_of(start, PIECE) for _, start in places]
        return starts, jnp.concatenate([xg[pl.ds(start, PIECE), :] for start in starts], axis=0)

    def add_down(starts, rows):
        wide = jnp.concatenate([grad_wide[pl.ds(start, PIECE), :] for start in starts], axis=0)
        down_sum[...] += lax.dot_general(
            wide, rows, contract_first, preferred_element_type=jnp.float32
        ).reshape(down_sum.shape)

    def body(group, carry):
        for step in range(len(STEPS)):
            @pl.when(group == (step if step < Z_GROUP else step + 1))
            def _():
                arrive(step)
                if step == Z_GROUP - 1:
                    for kind in (0, 1):
                        z_copy(kind, 1).wait_recv()
                if step + 2 < len(STEPS):
                    send(step + 2)

        @pl.when(group < GROUPS)
        def _():
            places = group_places(group)
            starts, rows = group_rows(places)
            product = jnp.dot(rows, w_v[...], preferred_element_type=jnp.float32)
            keep[group % 2] = product
            for pair in (0, 1):
                @pl.when(places[2 * pair][0] % 2 != core)
                def _():
                    slot = select(group, [slots[pair] for slots in SLOTS])
                    stage[slot] = product[pair * 2 * PIECE:(pair + 1) * 2 * PIECE].astype(jnp.bfloat16)
                    core_copy(slot).start()

        @pl.when(group > 0)
        def _():
            past = group - 1
            places = group_places(past)
            for pair in (0, 1):
                @pl.when(places[2 * pair][0] % 2 == core)
                def _():
                    slot = select(past, [slots[pair] for slots in SLOTS])
                    core_copy(slot).wait_recv()
                    for part in (0, 1):
                        plane, start = places[2 * pair + part]
                        number = start % (8 * SHARD) // PIECE
                        spot = pl.ds(pl.multiple_of(number * PIECE, PIECE), PIECE)
                        summed = (
                            keep[past % 2, pl.ds((2 * pair + part) * PIECE, PIECE), :]
                            + recv_core[slot, part * PIECE:(part + 1) * PIECE, :].astype(jnp.float32)
                        )

                        @pl.when(plane // 2 == z_hi)
                        def _():
                            total[spot, :] += summed

                        @pl.when(plane // 2 != z_hi)
                        def _():
                            z_stage[spot, :] = summed.astype(jnp.bfloat16)
                            far_copy(number).start()

        for at, work in enumerate(smalls):
            pl.when(group == at)(work)

        @pl.when((group >= CATCH_UP) & (group < GROUPS))
        def _():
            add_down(*group_rows(group_places(group)))

        @pl.when((group >= CATCH_UP) & (group < 2 * CATCH_UP))
        def _():
            add_down(*group_rows(group_places(group - CATCH_UP)))

        return carry

    lax.fori_loop(0, GROUPS + 1, body, 0)

    def moved_down(slot, carry):
        trial = keeper_ref[slot]
        new_down_ref[slot] = down_v[trial] - rate_ref[trial] * (down_sum[trial] * INV_WIDTH)
        return carry

    lax.fori_loop(0, TRIALS, moved_down, 0)

    def finish(number, carry):
        far_copy(number).wait_recv()
        spot = pl.ds(pl.multiple_of(number * PIECE, PIECE), PIECE)
        proj_ref[spot, :] = (total[spot, :] + recv_z[spot, :].astype(jnp.float32)).astype(jnp.bfloat16)
        return carry

    lax.fori_loop(0, 16, finish, 0)

    for step in range(len(STEPS)):
        every(step, lambda *what: sending(*what).wait_send())
    for kind in (0, 1):
        z_copy(kind, 0).wait_send()
    for name in SMALL:
        if not name.startswith("hid_x"):
            sends[name]().wait_send()

    @pl.when(x == row)
    def _():
        for name in trio("hid_x"):
            sends[name]().wait_send()

    def drain(number, carry):
        far_copy(number).wait_send()
        core_copy(number).wait_send()
        return carry

    lax.fori_loop(0, 16, drain, 0)


def per_device(
    packed_input_rows,
    frozen_weight,
    down_adapters,
    up_adapters,
    trial_learning_rates,
    row_trial_index,
    output_gradient,
    keeper_slot,
):
    width_in, width_out = frozen_weight.shape
    all_rows = row_trial_index.shape[0]
    block_rows = output_gradient.shape[0]
    vmem = pl.BlockSpec(memory_space=pltpu.VMEM)
    smem = pl.BlockSpec(memory_space=pltpu.SMEM)
    hbm = pl.BlockSpec(memory_space=pl.ANY)
    dma = pltpu.SemaphoreType.DMA
    f32, bf16 = jnp.float32, jnp.bfloat16
    half = TRIALS // 2
    return pl.pallas_call(
        whole_kernel,
        name="adapter_sweep",
        out_shape=(
            jax.ShapeDtypeStruct((block_rows, width_out), bf16),
            jax.ShapeDtypeStruct(down_adapters.shape, f32),
            jax.ShapeDtypeStruct(up_adapters.shape, f32),
        ),
        in_specs=[hbm, hbm, hbm, hbm, smem, vmem, hbm, smem],
        out_specs=(vmem, vmem, vmem),
        scratch_shapes=[
            pltpu.VMEM((all_rows, width_in), bf16),
            pltpu.VMEM((width_in, width_out), bf16),
            pltpu.VMEM((2, 4 * PIECE, width_out), f32),
            pltpu.VMEM((PAIRS, 2 * PIECE, width_out), bf16),
            pltpu.VMEM((PAIRS, 2 * PIECE, width_out), bf16),
            pltpu.VMEM((block_rows, width_out), f32),
            pltpu.VMEM((block_rows, width_out), bf16),
            pltpu.VMEM((block_rows, width_out), bf16),
            pltpu.VMEM(down_adapters.shape, f32),
            pltpu.VMEM((FLAT, width_in), bf16),
            pltpu.VMEM(up_adapters.shape, f32),
            pltpu.VMEM((FLAT, width_out), bf16),
            pltpu.VMEM((block_rows, width_out), bf16),
            pltpu.VMEM(down_adapters.shape, f32),
            pltpu.VMEM((all_rows, FLAT), bf16),
            pltpu.VMEM((block_rows, FLAT), bf16),
            pltpu.VMEM((RANK, SHARD), f32),
            pltpu.VMEM((RANK, SHARD), f32),
            pltpu.VMEM((RANK, SHARD), f32),
            pltpu.VMEM((RANK, SHARD), f32),
            pltpu.VMEM((32, RANK, SHARD), bf16),
            pltpu.VMEM((4, RANK, 256), f32),
            pltpu.VMEM((4, RANK, 256), f32),
            pltpu.VMEM((4, RANK, 256), f32),
            pltpu.VMEM((2, RANK, 256), f32),
            pltpu.VMEM((16, RANK, 256), bf16),
            pltpu.VMEM((TRIALS, RANK, width_out), f32),
            pltpu.VMEM((half, RANK, width_out), f32),
            pltpu.VMEM((half, RANK, width_out), f32),
            pltpu.VMEM((half, RANK, width_out), f32),
            pltpu.VMEM((TRIALS, RANK, width_out), f32),
            dma((5,)),
            dma((2, 2, len(ITEMS))),
            dma((2, 2, len(ITEMS))),
            dma((2,)),
            dma((2,)),
            dma((PAIRS,)),
            dma((PAIRS,)),
            dma((16,)),
            dma((16,)),
            dma((len(SMALL),)),
            dma((len(SMALL),)),
        ],
        compiler_params=pltpu.CompilerParams(
            collective_id=0, has_side_effects=True, vmem_limit_bytes=63 << 20
        ),
        cost_estimate=pl.CostEstimate(flops=22 * 10**9, bytes_accessed=20 << 20, transcendentals=0),
    )(
        packed_input_rows, frozen_weight, down_adapters, up_adapters, trial_learning_rates,
        row_trial_index.reshape(32, all_rows // 32), output_gradient, keeper_slot,
    )


def solution(mesh):
    in_specs = (
        P("col", "row"),
        P("row", "col"),
        P(None, None, "row"),
        P(None, None, "col"),
        P(),
        P(),
        P("row", "col"),
        P(),
    )
    out_specs = (P("row", "col"), P(None, None, "row"), P(None, None, "col"))
    return jax.shard_map(
        per_device, mesh=mesh, in_specs=in_specs, out_specs=out_specs, check_vma=False
    )
```

time: 608 us -> 128 us (0.21)
  waiting for transfers between devices: 337 us -> 0 us
  blocking collectives: 104 us -> 0 us
  between operations: 14.2 us -> 0.65 us
  other arithmetic: 8.05 us -> 0 us
    psum x2 -> x0, waiting for transfers between devices: 337 us -> none  [the longest x1 287 us: per_device(): lax.psum(own_trial(gradient_full, row * block_rows), 'col') * SCALE]
    all_gather x2 -> x0, blocking collectives: 87 us -> none  [the longest x1 74.9 us: per_device(): lax.all_gather(hidden.astype(jnp.bfloat16), 'col', axis=0, tiled=True)]
    psum x1 -> x0, blocking collectives: 17.4 us -> none  [per_device(): hidden = lax.psum(own_trial(hidden_full, col * SHARD), 'row') * INV_WIDTH]
  transfers between devices with their start and end apart: 2 -> 0, of which waited for: 2 -> 0; matrix products, arithmetic and copies ran while one was open for 0% -> 0% of each run, Pallas kernels for 0% -> 0%
where the time goes in v2:
time: 128 us; the launch traced here: 127 us
  Pallas kernels  121 us (95%)
  local copies, waits for them, and re-layouts  5.77 us (5%)
    pallas_call x1, Pallas kernels, per_device(): pl.pallas_call(whole_kernel, name='adapter_sweep', out_shape=(jax.ShapeDt...  121 us
    unnamed x7, local copies, waits for them, and re-layouts  5.77 us

profile of v2, /device:TPU:4, one launch (start us, length us, event | category | flops | bytes accessed | tf_op | source)
XLA Modules:
  0.0 127.3 jit_solution(4053623535273301643)
XLA Ops:
  0.6 120.9 %adapter_sweep.1 = (bf16[1024,896]{1,0:T(8,128)(2,1)}, f32[16,16,2048]{2,1,0:T(8,128)}, f32[16,16,896]{2,1,0:T(8,128)}) custom-call(bf16[128,2048]{1,0:T(8,128)(2,1)} %x_ref.1, bf16[2048,896]{1,0:T(8,128)(2,1)} %w_ref.1, f32[16,16,2048]{2,1,0:T(8,128)} %down_ref.1, f32[16,16,896]{2,1,0:T(8,128)} %up_ref.1, f32[16]{0:T(128)} %rate_ref.1, s32[32,128]{1,0:T(8,128)} %bitcast.1, ...), custom_call_target="tpu_custom_call" | custom-call | flops 22000001024 | bytes 20971520 | tf_op jit(solution)/shard_map/adapter_sweep/pallas_call | solution.py:554
  121.5 0.0 copy-start
  121.6 3.0 %copy.14 = bf16[1024,896]{1,0:T(8,128)(2,1)} copy(bf16[1024,896]{1,0:T(8,128)(2,1)} %get-tuple-element.6) | data formatting | bytes 3670016
  124.6 0.0 copy-done
  124.6 0.0 copy-start.1
  124.6 1.3 %copy.15 = f32[16,16,2048]{2,1,0:T(8,128)} copy(f32[16,16,2048]{2,1,0:T(8,128)S(1)} %copy-done) | data formatting | bytes 4194304
  125.9 0.5 copy-done.1
  126.4 0.9 copy.16
Async XLA Ops:
  121.5 3.0 %copy-start = (f32[16,16,2048]{2,1,0:T(8,128)S(1)}, f32[16,16,2048]{2,1,0:T(8,128)}, u32[]{:S(2)}) copy-start(f32[16,16,2048]{2,1,0:T(8,128)} %get-tuple-element.7) | copy-start | bytes 6291460
  124.6 1.8 %copy-start.1 = (f32[16,16,896]{2,1,0:T(8,128)S(1)}, f32[16,16,896]{2,1,0:T(8,128)}, u32[]{:S(2)}) copy-start(f32[16,16,896]{2,1,0:T(8,128)} %get-tuple-element.8) | copy-start | bytes 2752516

commit v3 on v2

--- a/solution.py
+++ b/solution.py
@@ -83,7 +83,8 @@
     + [f"grad_x{k}" for k in (1, 2, 3)] + [f"grad_y{k}" for k in (1, 2, 3)] + ["grad_z"]
     + [f"low_x{k}" for k in (1, 2, 3)] + ["low_core", "low_far", "up_core", "up_far", "up_share"]
 )
-CATCH_UP = 6
+FINISH, FINISH_LAG = 9, 3
+CATCH_UP = 11
 
 
 def select(index, values):
@@ -287,65 +288,91 @@
     )
     go("hid_core")
 
-    up_load.wait()
-    for trial in range(TRIALS):
-        up_low[trial * RANK:(trial + 1) * RANK, :] = up_v[trial].astype(jnp.bfloat16)
-    grad_load.wait()
-
-    def gradient_chunk(chunk, carry):
-        start = pl.multiple_of(chunk * 256, 256)
-        full = lax.dot_general(
-            up_low[...], grad_v[pl.ds(start, 256), :], contract_last, preferred_element_type=jnp.float32
-        )
-        grad_part[chunk] = pick_rank(full, row * 8 * SHARD + start)
-        return carry
-
-    lax.fori_loop(0, 4, gradient_chunk, 0)
-    go(*trio("grad_x"))
-    grad_x[x] = grad_part[x]
     down_sum[...] = jnp.zeros_like(down_sum)
     total[...] = jnp.zeros_like(total)
     weight_load.wait()
 
-    def small_0():
+    def hid_0():
         come("hid_core")
         hid_half[...] = hid_part[...] + hid_core[...]
         go("hid_far")
-        come(*trio("grad_x"))
-        grad_y[y] = (grad_x[0] + grad_x[1]) + (grad_x[2] + grad_x[3])
-        go(*trio("grad_y"))
-
-    def small_1():
+
+    def hid_1():
         come("hid_far")
         hid_low[col] = ((hid_half[...] + hid_far[...]) * INV_WIDTH).astype(jnp.bfloat16)
         go("hid_z")
-        come(*trio("grad_y"))
-        grad_z[z_lo] = (grad_y[0] + grad_y[1]) + (grad_y[2] + grad_y[3])
-        go("grad_z")
-
-    def small_2():
+
+    def hid_2():
         come("hid_z")
         go(*trio("hid_y"))
-        come("grad_z")
-        grad_low[row * 4 + x] = ((grad_z[0] + grad_z[1]) * SCALE).astype(jnp.bfloat16)
-        go(*trio("low_x"))
-
-    def small_3():
+
+    def hid_3():
         come(*trio("hid_y"))
 
         @pl.when(x == row)
         def _():
             go(*trio("hid_x"))
 
-        come(*trio("low_x"))
-        go("low_core")
-
-    def small_4():
+    def hid_4():
         for way in (1, 2, 3):
             @pl.when((x - way + 4) % 4 == row)
             def _():
                 sends[f"hid_x{way}"]().wait_recv()
 
+    def grad_0():
+        up_load.wait()
+        for trial in range(TRIALS):
+            up_low[trial * RANK:(trial + 1) * RANK, :] = up_v[trial].astype(jnp.bfloat16)
+        grad_load.wait()
+
+        def gradient_chunk(chunk, carry):
+            start = pl.multiple_of(chunk * 256, 256)
+            full = lax.dot_general(
+                up_low[...], grad_v[pl.ds(start, 256), :], contract_last, preferred_element_type=jnp.float32
+            )
+            grad_part[chunk] = pick_rank(full, row * 8 * SHARD + start)
+            return carry
+
+        lax.fori_loop(0, 4, gradient_chunk, 0)
+        grad_x[x] = grad_part[x]
+
+    def grad_1():
+        go(*trio("grad_x"))
+
+    def grad_2():
+        come(*trio("grad_x"))
+        grad_y[y] = (grad_x[0] + grad_x[1]) + (grad_x[2] + grad_x[3])
+        go(*trio("grad_y"))
+
+    def grad_3():
+        come(*trio("grad_y"))
+        grad_z[z_lo] = (grad_y[0] + grad_y[1]) + (grad_y[2] + grad_y[3])
+        go("grad_z")
+
+    def grad_4():
+        come("grad_z")
+        grad_low[row * 4 + x] = ((grad_z[0] + grad_z[1]) * SCALE).astype(jnp.bfloat16)
+        go(*trio("low_x"))
+
+    def grad_5():
+        come(*trio("low_x"))
+        go("low_core")
+
+    def grad_6():
+        come("low_core")
+        go("low_far")
+
+    def grad_7():
+        come("low_far")
+
+        def wide(chunk, carry):
+            start = pl.multiple_of(chunk * 256, 256)
+            grad_wide[pl.ds(start, 256), :] = widen(grad_low[chunk], start)
+            return carry
+
+        lax.fori_loop(0, 16, wide, 0)
+
+    def up_0():
         def wide(block, carry):
             start = pl.multiple_of(block * SHARD, SHARD)
             hid_wide[pl.ds(start, SHARD), :] = widen(hid_low[row * 8 + block], row * 8 * SHARD + start)
@@ -355,28 +382,18 @@
         full = lax.dot_general(hid_wide[...], grad_v[...], contract_first, preferred_element_type=jnp.float32)
         up_part[...] = full.reshape(up_part.shape)
         go("up_core")
-        come("low_core")
-        go("low_far")
-
-    def small_5():
+
+    def up_1():
         come("up_core")
         up_half[...] = up_part[half] + up_core[...]
         go("up_far")
-        come("low_far")
-
-        def wide(chunk, carry):
-            start = pl.multiple_of(chunk * 256, 256)
-            grad_wide[pl.ds(start, 256), :] = widen(grad_low[chunk], start)
-            return carry
-
-        lax.fori_loop(0, 16, wide, 0)
-
-    def small_6():
+
+    def up_2():
         come("up_far")
         up_sum[half] = up_half[...] + up_far[...]
         go("up_share")
 
-    def small_7():
+    def up_3():
         come("up_share")
 
         def moved(slot, carry):
@@ -386,7 +403,7 @@
 
         lax.fori_loop(0, TRIALS, moved, 0)
 
-    def small_8():
+    def adapter_term():
         def adapter(block, carry):
             spot = pl.ds(pl.multiple_of(block * SHARD, SHARD), SHARD)
             total[spot, :] += SCALE * jnp.dot(
@@ -396,7 +413,9 @@
 
         lax.fori_loop(0, 8, adapter, 0)
 
-    smalls = [small_0, small_1, small_2, small_3, small_4, small_5, small_6, small_7, small_8]
+    ahead = {0: [hid_0], 1: [hid_1, grad_1], 2: [hid_2], 3: [grad_2], 4: [hid_3], 5: [grad_3], 6: [hid_4, grad_4],
+             7: [up_1], 8: [grad_5], 9: [up_2, grad_6]}
+    after = {0: [grad_0], 6: [up_0], 8: [adapter_term], 10: [up_3], 11: [grad_7]}
 
     def decode(code):
         dx, dy, dz, kind = code % 4, code // 4 % 4, code // 16 % 2, code // 32
@@ -430,30 +449,19 @@
             wide, rows, contract_first, preferred_element_type=jnp.float32
         ).reshape(down_sum.shape)
 
+    def finish(group):
+        places = group_places(group)
+        for slot in range(4):
+            plane, start = places[slot]
+
+            @pl.when(plane == row)
+            def _():
+                number = start % (8 * SHARD) // PIECE
+                far_copy(number).wait_recv()
+                spot = pl.ds(pl.multiple_of(number * PIECE, PIECE), PIECE)
+                proj_ref[spot, :] = (total[spot, :] + recv_z[spot, :].astype(jnp.float32)).astype(jnp.bfloat16)
+
     def body(group, carry):
-        for step in range(len(STEPS)):
-            @pl.when(group == (step if step < Z_GROUP else step + 1))
-            def _():
-                arrive(step)
-                if step == Z_GROUP - 1:
-                    for kind in (0, 1):
-                        z_copy(kind, 1).wait_recv()
-                if step + 2 < len(STEPS):
-                    send(step + 2)
-
-        @pl.when(group < GROUPS)
-        def _():
-            places = group_places(group)
-            starts, rows = group_rows(places)
-            product = jnp.dot(rows, w_v[...], preferred_element_type=jnp.float32)
-            keep[group % 2] = product
-            for pair in (0, 1):
-                @pl.when(places[2 * pair][0] % 2 != core)
-                def _():
-                    slot = select(group, [slots[pair] for slots in SLOTS])
-                    stage[slot] = product[pair * 2 * PIECE:(pair + 1) * 2 * PIECE].astype(jnp.bfloat16)
-                    core_copy(slot).start()
-
         @pl.when(group > 0)
         def _():
             past = group - 1
@@ -481,16 +489,64 @@
                             z_stage[spot, :] = summed.astype(jnp.bfloat16)
                             far_copy(number).start()
 
-        for at, work in enumerate(smalls):
-            pl.when(group == at)(work)
+        @pl.when(group == Z_GROUP)
+        def _():
+            for work in ahead.get(Z_GROUP, ()):
+                work()
+
+        for step in range(len(STEPS)):
+            @pl.when(group == (step if step < Z_GROUP else step + 1))
+            def _():
+                arrive(step)
+                if step == Z_GROUP - 1:
+                    for kind in (0, 1):
+                        z_copy(kind, 1).wait_recv()
+                for work in ahead.get(step if step < Z_GROUP else step + 1, ()):
+                    work()
+                if step + 2 < len(STEPS):
+                    send(step + 2)
+
+        @pl.when(group < GROUPS)
+        def _():
+            places = group_places(group)
+            starts, rows = group_rows(places)
+            product = jnp.dot(rows, w_v[...], preferred_element_type=jnp.float32)
+            keep[group % 2] = product
+            for pair in (0, 1):
+                @pl.when(places[2 * pair][0] % 2 != core)
+                def _():
+                    slot = select(group, [slots[pair] for slots in SLOTS])
+                    stage[slot] = product[pair * 2 * PIECE:(pair + 1) * 2 * PIECE].astype(jnp.bfloat16)
+                    core_copy(slot).start()
+
+        for at, works in after.items():
+            @pl.when(group == at)
+            def _():
+                for work in works:
+                    work()
 
         @pl.when((group >= CATCH_UP) & (group < GROUPS))
         def _():
             add_down(*group_rows(group_places(group)))
 
-        @pl.when((group >= CATCH_UP) & (group < 2 * CATCH_UP))
+            def earlier(number, carry):
+                before = (group - CATCH_UP) * 3 + number
+
+                @pl.when(before < CATCH_UP)
+                def _():
+                    add_down(*group_rows(group_places(before)))
+
+                return carry
+
+            lax.fori_loop(0, 3, earlier, 0)
+
+        @pl.when(group >= FINISH)
         def _():
-            add_down(*group_rows(group_places(group - CATCH_UP)))
+            finish(group - FINISH_LAG)
+
+        @pl.when((group >= FINISH) & (group < 2 * FINISH - FINISH_LAG))
+        def _():
+            finish(group - FINISH)
 
         return carry
 
@@ -503,13 +559,11 @@
 
     lax.fori_loop(0, TRIALS, moved_down, 0)
 
-    def finish(number, carry):
-        far_copy(number).wait_recv()
-        spot = pl.ds(pl.multiple_of(number * PIECE, PIECE), PIECE)
-        proj_ref[spot, :] = (total[spot, :] + recv_z[spot, :].astype(jnp.float32)).astype(jnp.bfloat16)
+    def last(group, carry):
+        finish(group)
         return carry
 
-    lax.fori_loop(0, 16, finish, 0)
+    lax.fori_loop(GROUPS - FINISH_LAG + 1, GROUPS, last, 0)
 
     for step in range(len(STEPS)):
         every(step, lambda *what: sending(*what).wait_send())
@@ -530,6 +584,15 @@
         return carry
 
     lax.fori_loop(0, 16, drain, 0)
+
+
+def write_out(*refs):
+    sources, targets, sems = refs[:3], refs[3:6], refs[6]
+    copies = [pltpu.make_async_copy(sources[at], targets[at], sems.at[at]) for at in range(3)]
+    for copy in copies:
+        copy.start()
+    for copy in copies:
+        copy.wait()
 
 
 def per_device(
@@ -551,13 +614,13 @@
     dma = pltpu.SemaphoreType.DMA
     f32, bf16 = jnp.float32, jnp.bfloat16
     half = TRIALS // 2
-    return pl.pallas_call(
+    held = pl.pallas_call(
         whole_kernel,
         name="adapter_sweep",
         out_shape=(
-            jax.ShapeDtypeStruct((block_rows, width_out), bf16),
-            jax.ShapeDtypeStruct(down_adapters.shape, f32),
-            jax.ShapeDtypeStruct(up_adapters.shape, f32),
+            pltpu.VMEM((block_rows, width_out), bf16),
+            pltpu.VMEM(down_adapters.shape, f32),
+            pltpu.VMEM(up_adapters.shape, f32),
         ),
         in_specs=[hbm, hbm, hbm, hbm, smem, vmem, hbm, smem],
         out_specs=(vmem, vmem, vmem),
@@ -606,13 +669,23 @@
             dma((len(SMALL),)),
         ],
         compiler_params=pltpu.CompilerParams(
-            collective_id=0, has_side_effects=True, vmem_limit_bytes=63 << 20
+            collective_id=0, has_side_effects=True, vmem_limit_bytes=56 << 20
         ),
         cost_estimate=pl.CostEstimate(flops=22 * 10**9, bytes_accessed=20 << 20, transcendentals=0),
     )(
         packed_input_rows, frozen_weight, down_adapters, up_adapters, trial_learning_rates,
         row_trial_index.reshape(32, all_rows // 32), output_gradient, keeper_slot,
     )
+    held = [pltpu.with_memory_space_constraint(array, pltpu.VMEM) for array in held]
+    return tuple(pl.pallas_call(
+        write_out,
+        name="write_out",
+        out_shape=tuple(jax.ShapeDtypeStruct(array.shape, array.dtype) for array in held),
+        in_specs=[vmem] * len(held),
+        out_specs=tuple([hbm] * len(held)),
+        scratch_shapes=[dma((len(held),))],
+        compiler_params=pltpu.CompilerParams(vmem_limit_bytes=1 << 20),
+    )(*held))
 
 
 def solution(mesh):

time: 128 us -> 110 us (0.86)
  Pallas kernels: 121 us -> 110 us
  local copies, waits for them, and re-layouts: 5.77 us -> 0 us
    pallas_call x1 -> x2, Pallas kernels: 121 us -> 110 us  [the longest x1 107 us: per_device(): pl.pallas_call(whole_kernel, name='adapter_sweep', out_shape=(pltpu.VMEM(...]
    unnamed x7 -> x0, local copies, waits for them, and re-layouts: 5.77 us -> none
where the time goes in v3:
time: 110 us
  Pallas kernels  110 us (100%)
    pallas_call x1, Pallas kernels, per_device(): pl.pallas_call(whole_kernel, name='adapter_sweep', out_shape=(pltpu.VMEM(...  107 us
    pallas_call x1, Pallas kernels, per_device(): pl.pallas_call(write_out, name='write_out', out_shape=tuple((jax.ShapeDty...  2.24 us

profile of v3, /device:TPU:4, one launch (start us, length us, event | category | flops | bytes accessed | tf_op | source)
XLA Modules:
  0.0 110.3 jit_solution(894489666681732438)
XLA Ops:
  0.6 107.4 %adapter_sweep.1 = (bf16[1024,896]{1,0:T(8,128)(2,1)S(1)}, f32[16,16,2048]{2,1,0:T(8,128)S(1)}, f32[16,16,896]{2,1,0:T(8,128)S(1)}) custom-call(bf16[128,2048]{1,0:T(8,128)(2,1)} %x_ref.1, bf16[2048,896]{1,0:T(8,128)(2,1)} %w_ref.1, f32[16,16,2048]{2,1,0:T(8,128)} %down_ref.1, f32[16,16,896]{2,1,0:T(8,128)} %up_ref.1, f32[16]{0:T(128)} %rate_ref.1, ...), custom_call_target="tpu_custom_call" | custom-call | flops 22000001024 | bytes 20971520 | tf_op jit(solution)/shard_map/adapter_sweep/pallas_call | solution.py:617
  108.1 2.2 %write_out.1 = (bf16[1024,896]{1,0:T(8,128)(2,1)}, f32[16,16,2048]{2,1,0:T(8,128)}, f32[16,16,896]{2,1,0:T(8,128)}) custom-call(bf16[1024,896]{1,0:T(8,128)(2,1)S(1)} %get-tuple-element.6.refs_0_, f32[16,16,2048]{2,1,0:T(8,128)S(1)} %get-tuple-element.7.refs_1_, f32[16,16,896]{2,1,0:T(8,128)S(1)} %get-tuple-element.8.refs_2_), custom_call_target="tpu_custom_call" | custom-call | tf_op jit(solution)/shard_map/write_out/pallas_call | solution.py:680

commit v4 on v3

--- a/solution.py
+++ b/solution.py
@@ -17,25 +17,47 @@
 INV_WIDTH = D ** (-0.5)
 
 STEPS = (
-    (("F", 0),),
-    (("L", 0, 0),),
-    (("L", 1, 0),),
-    (("RF", 0), ("RL", 0, 0)),
-    (("F", 1),),
-    (("L", 0, 1),),
-    (("L", 3, 0),),
-    (("L", 2, 0),),
-    (("RF", 1), ("RL", 0, 1)),
-    (("RL", 1, 0), ("RL", 3, 0)),
-    (("L", 1, 1),),
-    (("L", 3, 1),),
-    (("L", 2, 1),),
-    (("RL", 1, 1), ("RL", 3, 1)),
-    (("RL", 2, 0), ("RL", 2, 1)),
+    (
+        (("F", 0),),
+        (("L", 0, 0),),
+        (("L", 1, 0),),
+        (("RF", 0), ("RL", 0, 0)),
+        (("L", 3, 0),),
+        (("L", 0, 1),),
+        (("L", 2, 0),),
+        (("F", 1),),
+        (("RL", 1, 0), ("RL", 3, 0)),
+        (("L", 2, 1),),
+        (("L", 3, 1),),
+        (("RL", 0, 1), ("RL", 2, 0)),
+        (("L", 1, 1),),
+        (("RL", 2, 1), ("RL", 3, 1)),
+        (("RL", 1, 1),),
+    ),
+    (
+        (("F", 0),),
+        (("L", 0, 0),),
+        (("L", 1, 0),),
+        (("RF", 0), ("RL", 0, 0)),
+        (("L", 3, 0),),
+        (("L", 0, 1),),
+        (("L", 2, 0),),
+        (("F", 1),),
+        (("RL", 1, 0), ("RL", 3, 0)),
+        (("L", 2, 1),),
+        (("L", 1, 1),),
+        (("RL", 2, 0), ("RL", 2, 1)),
+        (("L", 3, 1),),
+        (("RL", 0, 1), ("RL", 1, 1)),
+        (("RL", 3, 1),),
+    ),
 )
-ITEMS = tuple(item for step in STEPS for item in step)
+ITEMS = tuple(item for step in STEPS[0] for item in step)
+COUNT = len(STEPS[0])
+SWAP_SENT, SWAP_USED = 2, 5
 Z_GROUP = 3
-GROUPS = len(STEPS) + 1
+GROUPS = COUNT
+TURN = [step + (step >= Z_GROUP) for step in range(COUNT)]
 
 
 def offsets(kind, first, last, zz):
@@ -46,7 +68,7 @@
     name, zz = item[0], item[-1]
     kind = axis if name in ("F", "RF") else 1 - axis
     if name == "F":
-        return [offsets(kind, 3, 0, zz), offsets(kind, 1, 0, zz)]
+        return [offsets(kind, 3, 0, zz), offsets(kind, 2 if zz else 1, 0, zz)]
     if name == "RF":
         return [offsets(kind, 2, 0, zz)]
     if name == "L":
@@ -56,35 +78,38 @@
 
 def group_pieces():
     groups = []
-    for step in STEPS:
-        groups.append([piece for axis in (0, 1) for item in step for piece in landed(axis, item)])
+    for step in range(COUNT):
+        groups.append([
+            piece for axis in (0, 1) for item in STEPS[axis][step] for piece in landed(axis, item)
+        ])
     groups.insert(Z_GROUP, [(0, 0, 0, 0), (0, 0, 1, 0), (0, 0, 0, 1), (0, 0, 1, 1)])
+    groups[-1] = [offsets(kind, 1, 0, 1) for kind in (0, 1)] + groups[-1]
     return groups
 
 
 CODES = [[dx + 4 * dy + 16 * dz + 32 * kind for dx, dy, dz, kind in group] for group in group_pieces()]
 
 
-def pair_slots():
+def piece_slots():
     seen, slots = [0, 0], []
     for group in group_pieces():
         slots.append([])
-        for pair in (0, 1):
-            odd = group[2 * pair][0] % 2
+        for piece in group:
+            odd = piece[0] % 2
             slots[-1].append(seen[odd])
             seen[odd] += 1
     return slots
 
 
-SLOTS = pair_slots()
-PAIRS = 16
+SLOTS = piece_slots()
+SENT = 32
 SMALL = (
     ["hid_core", "hid_far", "hid_z"] + [f"hid_y{k}" for k in (1, 2, 3)] + [f"hid_x{k}" for k in (1, 2, 3)]
     + [f"grad_x{k}" for k in (1, 2, 3)] + [f"grad_y{k}" for k in (1, 2, 3)] + ["grad_z"]
     + [f"low_x{k}" for k in (1, 2, 3)] + ["low_core", "low_far", "up_core", "up_far", "up_share"]
 )
-FINISH, FINISH_LAG = 9, 3
-CATCH_UP = 11
+FINISH, FINISH_LAG = 10, 5
+CATCH_UP, CATCH_EACH = 11, 2
 
 
 def select(index, values):
@@ -97,12 +122,12 @@
 def whole_kernel(
     x_ref, w_ref, down_ref, up_ref, rate_ref, trial_ref, grad_ref, keeper_ref,
     proj_ref, new_down_ref, new_up_ref,
-    xg, w_v, keep, stage, recv_core, total, z_stage, recv_z,
+    xg, w_v, keep, keep_half, stage, recv_core, total, z_stage, recv_z,
     down_v, down_low, up_v, up_low, grad_v, down_sum, grad_wide, hid_wide,
     hid_part, hid_core, hid_half, hid_far, hid_low,
-    grad_part, grad_x, grad_y, grad_z, grad_low,
+    grad_part, grad_sum, grad_x, grad_y, grad_z, grad_low,
     up_part, up_core, up_half, up_far, up_sum,
-    local_sem, send_sem, recv_sem, z_send, z_recv, core_send, core_recv, far_send, far_recv,
+    local_sem, send_sem, recv_sem, z_send, z_recv, swap_send, swap_recv, core_send, core_recv, far_send, far_recv,
     small_send, small_recv,
 ):
     row = lax.axis_index("row")
@@ -154,7 +179,7 @@
         kind = axis if name in ("F", "RF") else 1 - axis
         back = 3 if way == 0 else 1
         if name == "F":
-            start, rows = base(offsets(kind, 0, 0, zz)), PIECE
+            start, rows = base(offsets(kind, way if zz else 0, 0, zz)), PIECE
         elif name == "RF":
             start, rows = base(offsets(kind, back, 0, zz)) + way * HALF, HALF
         elif name == "L":
@@ -180,8 +205,8 @@
         )
 
     def every(step, action):
-        for item in STEPS[step]:
-            for axis in (0, 1):
+        for axis in (0, 1):
+            for item in STEPS[axis][step]:
                 for way in (0, 1):
                     action(axis, way, item)
 
@@ -193,6 +218,9 @@
 
     def z_copy(kind, dz):
         return remote(base((0, 0, dz, kind)), PIECE, z_send.at[kind], z_recv.at[kind], z_mate)
+
+    def swap(kind, dz):
+        return remote(base(offsets(kind, 1, 0, dz)), PIECE, swap_send.at[kind], swap_recv.at[kind], z_mate)
 
     send(0)
     for kind in (0, 1):
@@ -212,7 +240,7 @@
         "hid_core": lambda: small("hid_core", hid_part, hid_core, core_mate),
         "hid_far": lambda: small("hid_far", hid_half, hid_far, far_mate),
         "hid_z": lambda: small("hid_z", hid_low.at[col], hid_low.at[col], z_mate),
-        "grad_z": lambda: small("grad_z", grad_z.at[z_lo], grad_z.at[z_lo], z_mate),
+        "grad_z": lambda: small("grad_z", grad_part, grad_z, z_mate),
         "low_core": lambda: small(
             "low_core", grad_low.at[pl.ds(row * 4, 4)], grad_low.at[pl.ds(row * 4, 4)], core_mate),
         "low_far": lambda: small(
@@ -228,7 +256,7 @@
             sends[f"hid_y{way}"] = lambda: small(f"hid_y{way}", hid_low.at[block], hid_low.at[block], to_y)
             sends[f"hid_x{way}"] = lambda: small(f"hid_x{way}", hid_low.at[plane], hid_low.at[plane], to_x)
             sends[f"grad_x{way}"] = lambda: small(
-                f"grad_x{way}", grad_part.at[(x + way) % 4], grad_x.at[x], to_x)
+                f"grad_x{way}", grad_sum.at[(x + way) % 4], grad_x.at[x], to_x)
             sends[f"grad_y{way}"] = lambda: small(f"grad_y{way}", grad_y.at[y], grad_y.at[y], to_y)
             own_chunk = row * 4 + x
             sends[f"low_x{way}"] = lambda: small(
@@ -334,10 +362,12 @@
             return carry
 
         lax.fori_loop(0, 4, gradient_chunk, 0)
-        grad_x[x] = grad_part[x]
 
     def grad_1():
+        come("grad_z")
+        grad_sum[...] = grad_part[...] + grad_z[...]
         go(*trio("grad_x"))
+        grad_x[x] = grad_sum[x]
 
     def grad_2():
         come(*trio("grad_x"))
@@ -346,31 +376,33 @@
 
     def grad_3():
         come(*trio("grad_y"))
-        grad_z[z_lo] = (grad_y[0] + grad_y[1]) + (grad_y[2] + grad_y[3])
-        go("grad_z")
+        gradient = (grad_y[0] + grad_y[1]) + (grad_y[2] + grad_y[3])
+        grad_low[row * 4 + x] = (gradient * SCALE).astype(jnp.bfloat16)
+        go(*trio("low_x"))
 
     def grad_4():
-        come("grad_z")
-        grad_low[row * 4 + x] = ((grad_z[0] + grad_z[1]) * SCALE).astype(jnp.bfloat16)
-        go(*trio("low_x"))
-
-    def grad_5():
         come(*trio("low_x"))
         go("low_core")
 
-    def grad_6():
+    def grad_5():
         come("low_core")
         go("low_far")
 
-    def grad_7():
-        come("low_far")
-
-        def wide(chunk, carry):
+    def widen_gradient(side):
+        def wide(number, carry):
+            chunk = side * 8 + number
             start = pl.multiple_of(chunk * 256, 256)
             grad_wide[pl.ds(start, 256), :] = widen(grad_low[chunk], start)
             return carry
 
-        lax.fori_loop(0, 16, wide, 0)
+        lax.fori_loop(0, 8, wide, 0)
+
+    def grad_6():
+        widen_gradient(z_hi)
+
+    def grad_7():
+        come("low_far")
+        widen_gradient(1 - z_hi)
 
     def up_0():
         def wide(block, carry):
@@ -385,12 +417,12 @@
 
     def up_1():
         come("up_core")
-        up_half[...] = up_part[half] + up_core[...]
+        up_half[...] = (up_part[half] + up_core[...]).astype(jnp.bfloat16)
         go("up_far")
 
     def up_2():
         come("up_far")
-        up_sum[half] = up_half[...] + up_far[...]
+        up_sum[half] = up_half[...].astype(jnp.float32) + up_far[...].astype(jnp.float32)
         go("up_share")
 
     def up_3():
@@ -413,9 +445,11 @@
 
         lax.fori_loop(0, 8, adapter, 0)
 
-    ahead = {0: [hid_0], 1: [hid_1, grad_1], 2: [hid_2], 3: [grad_2], 4: [hid_3], 5: [grad_3], 6: [hid_4, grad_4],
-             7: [up_1], 8: [grad_5], 9: [up_2, grad_6]}
-    after = {0: [grad_0], 6: [up_0], 8: [adapter_term], 10: [up_3], 11: [grad_7]}
+    ahead = {0: [hid_0], 2: [hid_1, grad_1], 4: [hid_2, grad_2], 6: [hid_3, grad_3], 8: [hid_4, grad_4],
+             9: [up_1, grad_5], 11: [up_2]}
+    after = {7: [], 8: [up_0], 9: [grad_6], 10: [adapter_term], 11: [grad_7], 12: [up_3]}
+    grad_0()
+    go("grad_z")
 
     def decode(code):
         dx, dy, dz, kind = code % 4, code // 4 % 4, code // 16 % 2, code // 32
@@ -461,63 +495,80 @@
                 spot = pl.ds(pl.multiple_of(number * PIECE, PIECE), PIECE)
                 proj_ref[spot, :] = (total[spot, :] + recv_z[spot, :].astype(jnp.float32)).astype(jnp.bfloat16)
 
+    def add_core(place, own_sum, slot):
+        plane, start = place
+        number = start % (8 * SHARD) // PIECE
+        spot = pl.ds(pl.multiple_of(number * PIECE, PIECE), PIECE)
+        summed = own_sum + recv_core[slot].astype(jnp.float32)
+
+        @pl.when(plane // 2 == z_hi)
+        def _():
+            total[spot, :] += summed
+
+        @pl.when(plane // 2 != z_hi)
+        def _():
+            z_stage[spot, :] = summed.astype(jnp.bfloat16)
+            far_copy(number).start()
+
+    def hand_over(places, slots, product):
+        for at, (plane, _) in enumerate(places):
+            @pl.when(plane % 2 != core)
+            def _():
+                stage[slots[at]] = product[at * PIECE:(at + 1) * PIECE].astype(jnp.bfloat16)
+                core_copy(slots[at]).start()
+
+    def take_over(places, slots, own_sums):
+        for at, place in enumerate(places):
+            @pl.when(place[0] % 2 == core)
+            def _():
+                core_copy(slots[at]).wait_recv()
+                add_core(place, own_sums[at * PIECE:(at + 1) * PIECE, :], slots[at])
+
+    extra_places = group_places(GROUPS)
+
+    def extra_product(part):
+        places, slots = extra_places[2 * part:2 * part + 2], SLOTS[GROUPS][2 * part:2 * part + 2]
+        _, rows = group_rows(places)
+        product = jnp.dot(rows, w_v[...], preferred_element_type=jnp.float32)
+        keep_half[...] = product
+        hand_over(places, slots, product)
+
+    def extra_sum(part):
+        take_over(extra_places[2 * part:2 * part + 2], SLOTS[GROUPS][2 * part:2 * part + 2], keep_half)
+
+    after[7].append(lambda: extra_product(0))
+    after[8].insert(0, lambda: extra_sum(0))
+
     def body(group, carry):
-        @pl.when(group > 0)
-        def _():
-            past = group - 1
-            places = group_places(past)
-            for pair in (0, 1):
-                @pl.when(places[2 * pair][0] % 2 == core)
-                def _():
-                    slot = select(past, [slots[pair] for slots in SLOTS])
-                    core_copy(slot).wait_recv()
-                    for part in (0, 1):
-                        plane, start = places[2 * pair + part]
-                        number = start % (8 * SHARD) // PIECE
-                        spot = pl.ds(pl.multiple_of(number * PIECE, PIECE), PIECE)
-                        summed = (
-                            keep[past % 2, pl.ds((2 * pair + part) * PIECE, PIECE), :]
-                            + recv_core[slot, part * PIECE:(part + 1) * PIECE, :].astype(jnp.float32)
-                        )
-
-                        @pl.when(plane // 2 == z_hi)
-                        def _():
-                            total[spot, :] += summed
-
-                        @pl.when(plane // 2 != z_hi)
-                        def _():
-                            z_stage[spot, :] = summed.astype(jnp.bfloat16)
-                            far_copy(number).start()
-
         @pl.when(group == Z_GROUP)
         def _():
             for work in ahead.get(Z_GROUP, ()):
                 work()
 
-        for step in range(len(STEPS)):
-            @pl.when(group == (step if step < Z_GROUP else step + 1))
+        for step in range(COUNT - 1):
+            @pl.when(group == TURN[step])
             def _():
                 arrive(step)
                 if step == Z_GROUP - 1:
                     for kind in (0, 1):
                         z_copy(kind, 1).wait_recv()
-                for work in ahead.get(step if step < Z_GROUP else step + 1, ()):
+                if step == SWAP_USED:
+                    for kind in (0, 1):
+                        swap(kind, 1).wait_recv()
+                for work in ahead.get(TURN[step], ()):
                     work()
-                if step + 2 < len(STEPS):
+                if step + 2 < COUNT:
                     send(step + 2)
-
-        @pl.when(group < GROUPS)
-        def _():
-            places = group_places(group)
-            starts, rows = group_rows(places)
-            product = jnp.dot(rows, w_v[...], preferred_element_type=jnp.float32)
-            keep[group % 2] = product
-            for pair in (0, 1):
-                @pl.when(places[2 * pair][0] % 2 != core)
-                def _():
-                    slot = select(group, [slots[pair] for slots in SLOTS])
-                    stage[slot] = product[pair * 2 * PIECE:(pair + 1) * 2 * PIECE].astype(jnp.bfloat16)
-                    core_copy(slot).start()
+                if step == SWAP_SENT:
+                    for kind in (0, 1):
+                        swap(kind, 0).start()
+
+        places = group_places(group)
+        starts, rows = group_rows(places)
+        product = jnp.dot(rows, w_v[...], preferred_element_type=jnp.float32)
+        keep[...] = product
+        slots = [select(group, [each[at] for each in SLOTS]) for at in range(4)]
+        hand_over(places, slots, product)
 
         for at, works in after.items():
             @pl.when(group == at)
@@ -525,32 +576,39 @@
                 for work in works:
                     work()
 
-        @pl.when((group >= CATCH_UP) & (group < GROUPS))
+        @pl.when(group >= CATCH_UP)
         def _():
             add_down(*group_rows(group_places(group)))
 
+        take_over(places, slots, keep)
+
+        @pl.when(group >= CATCH_UP)
+        def _():
             def earlier(number, carry):
-                before = (group - CATCH_UP) * 3 + number
-
-                @pl.when(before < CATCH_UP)
-                def _():
-                    add_down(*group_rows(group_places(before)))
-
+                add_down(*group_rows(group_places((group - CATCH_UP) * CATCH_EACH + number)))
                 return carry
 
-            lax.fori_loop(0, 3, earlier, 0)
+            lax.fori_loop(0, CATCH_EACH, earlier, 0)
 
         @pl.when(group >= FINISH)
         def _():
             finish(group - FINISH_LAG)
-
-        @pl.when((group >= FINISH) & (group < 2 * FINISH - FINISH_LAG))
-        def _():
             finish(group - FINISH)
 
         return carry
 
-    lax.fori_loop(0, GROUPS + 1, body, 0)
+    lax.fori_loop(0, GROUPS, body, 0)
+
+    arrive(COUNT - 1)
+    extra_product(1)
+    add_down(*group_rows(extra_places))
+    extra_sum(1)
+
+    def rest(group, carry):
+        add_down(*group_rows(group_places(group)))
+        return carry
+
+    lax.fori_loop((GROUPS - CATCH_UP) * CATCH_EACH, CATCH_UP, rest, 0)
 
     def moved_down(slot, carry):
         trial = keeper_ref[slot]
@@ -563,10 +621,12 @@
         finish(group)
         return carry
 
-    lax.fori_loop(GROUPS - FINISH_LAG + 1, GROUPS, last, 0)
-
-    for step in range(len(STEPS)):
+    lax.fori_loop(GROUPS - FINISH_LAG, GROUPS + 1, last, 0)
+
+    for step in range(COUNT):
         every(step, lambda *what: sending(*what).wait_send())
+    for kind in (0, 1):
+        swap(kind, 0).wait_send()
     for kind in (0, 1):
         z_copy(kind, 0).wait_send()
     for name in SMALL:
@@ -579,11 +639,15 @@
             sends[name]().wait_send()
 
     def drain(number, carry):
-        far_copy(number).wait_send()
         core_copy(number).wait_send()
         return carry
 
-    lax.fori_loop(0, 16, drain, 0)
+    def drain_far(number, carry):
+        far_copy(number).wait_send()
+        return carry
+
+    lax.fori_loop(0, SENT, drain, 0)
+    lax.fori_loop(0, 16, drain_far, 0)
 
 
 def write_out(*refs):
@@ -627,9 +691,10 @@
         scratch_shapes=[
             pltpu.VMEM((all_rows, width_in), bf16),
             pltpu.VMEM((width_in, width_out), bf16),
-            pltpu.VMEM((2, 4 * PIECE, width_out), f32),
-            pltpu.VMEM((PAIRS, 2 * PIECE, width_out), bf16),
-            pltpu.VMEM((PAIRS, 2 * PIECE, width_out), bf16),
+            pltpu.VMEM((4 * PIECE, width_out), f32),
+            pltpu.VMEM((2 * PIECE, width_out), f32),
+            pltpu.VMEM((SENT, PIECE, width_out), bf16),
+            pltpu.VMEM((SENT, PIECE, width_out), bf16),
             pltpu.VMEM((block_rows, width_out), f32),
             pltpu.VMEM((block_rows, width_out), bf16),
             pltpu.VMEM((block_rows, width_out), bf16),
@@ -649,20 +714,23 @@
             pltpu.VMEM((4, RANK, 256), f32),
             pltpu.VMEM((4, RANK, 256), f32),
             pltpu.VMEM((4, RANK, 256), f32),
-            pltpu.VMEM((2, RANK, 256), f32),
+            pltpu.VMEM((4, RANK, 256), f32),
+            pltpu.VMEM((4, RANK, 256), f32),
             pltpu.VMEM((16, RANK, 256), bf16),
             pltpu.VMEM((TRIALS, RANK, width_out), f32),
             pltpu.VMEM((half, RANK, width_out), f32),
-            pltpu.VMEM((half, RANK, width_out), f32),
-            pltpu.VMEM((half, RANK, width_out), f32),
+            pltpu.VMEM((half, RANK, width_out), bf16),
+            pltpu.VMEM((half, RANK, width_out), bf16),
             pltpu.VMEM((TRIALS, RANK, width_out), f32),
             dma((5,)),
             dma((2, 2, len(ITEMS))),
             dma((2, 2, len(ITEMS))),
             dma((2,)),
             dma((2,)),
-            dma((PAIRS,)),
-            dma((PAIRS,)),
+            dma((2,)),
+            dma((2,)),
+            dma((SENT,)),
+            dma((SENT,)),
             dma((16,)),
             dma((16,)),
             dma((len(SMALL),)),

time: 110 us -> 107 us (0.973); the launches traced: 110 us -> 106 us
  Pallas kernels: 110 us -> 105 us
    pallas_call x1, Pallas kernels: 107 us -> 103 us  [per_device(): pl.pallas_call(whole_kernel, name='adapter_sweep', out_shape=(pltpu.VMEM(...]
where the time goes in v4:
time: 107 us; the launch traced here: 106 us
  Pallas kernels  105 us (98%)
    pallas_call x1, Pallas kernels, per_device(): pl.pallas_call(whole_kernel, name='adapter_sweep', out_shape=(pltpu.VMEM(...  103 us
    pallas_call x1, Pallas kernels, per_device(): pl.pallas_call(write_out, name='write_out', out_shape=tuple((jax.ShapeDty...  2.24 us

profile of v4, /device:TPU:4, one launch (start us, length us, event | category | flops | bytes accessed | tf_op | source)
XLA Modules:
  0.0 105.8 jit_solution(3198665911695599163)
XLA Ops:
  0.6 102.9 %adapter_sweep.1 = (bf16[1024,896]{1,0:T(8,128)(2,1)S(1)}, f32[16,16,2048]{2,1,0:T(8,128)S(1)}, f32[16,16,896]{2,1,0:T(8,128)S(1)}) custom-call(bf16[128,2048]{1,0:T(8,128)(2,1)} %x_ref.1, bf16[2048,896]{1,0:T(8,128)(2,1)} %w_ref.1, f32[16,16,2048]{2,1,0:T(8,128)} %down_ref.1, f32[16,16,896]{2,1,0:T(8,128)} %up_ref.1, f32[16]{0:T(128)} %rate_ref.1, ...), custom_call_target="tpu_custom_call" | custom-call | flops 22000001024 | bytes 20971520 | tf_op jit(solution)/shard_map/adapter_sweep/pallas_call | solution.py:681
  103.5 2.2 %write_out.1 = (bf16[1024,896]{1,0:T(8,128)(2,1)}, f32[16,16,2048]{2,1,0:T(8,128)}, f32[16,16,896]{2,1,0:T(8,128)}) custom-call(bf16[1024,896]{1,0:T(8,128)(2,1)S(1)} %get-tuple-element.6.refs_0_, f32[16,16,2048]{2,1,0:T(8,128)S(1)} %get-tuple-element.7.refs_1_, f32[16,16,896]{2,1,0:T(8,128)S(1)} %get-tuple-element.8.refs_2_), custom_call_target="tpu_custom_call" | custom-call | tf_op jit(solution)/shard_map/write_out/pallas_call | solution.py:748

commit v5 on v4

--- a/solution.py
+++ b/solution.py
@@ -108,8 +108,8 @@
     + [f"grad_x{k}" for k in (1, 2, 3)] + [f"grad_y{k}" for k in (1, 2, 3)] + ["grad_z"]
     + [f"low_x{k}" for k in (1, 2, 3)] + ["low_core", "low_far", "up_core", "up_far", "up_share"]
 )
-FINISH, FINISH_LAG = 10, 5
-CATCH_UP, CATCH_EACH = 11, 2
+FINISH, FINISH_EACH, FINISHED = 11, 3, 9
+CATCH_UP, CATCH_EACH = 10, 3
 
 
 def select(index, values):
@@ -213,6 +213,9 @@
     def send(step):
         every(step, lambda *what: sending(*what).start())
 
+    def sent(step):
+        every(step, lambda *what: sending(*what).wait_send())
+
     def arrive(step):
         every(step, lambda *what: receiving(*what).wait_recv())
 
@@ -234,12 +237,13 @@
             device_id=mate, device_id_type=MESH,
         )
 
+    own_slot = y * 2 + z_lo
     half = pl.ds(core * (TRIALS // 2), TRIALS // 2)
     other_half = pl.ds((1 - core) * (TRIALS // 2), TRIALS // 2)
     sends = {
         "hid_core": lambda: small("hid_core", hid_part, hid_core, core_mate),
         "hid_far": lambda: small("hid_far", hid_half, hid_far, far_mate),
-        "hid_z": lambda: small("hid_z", hid_low.at[col], hid_low.at[col], z_mate),
+        "hid_z": lambda: small("hid_z", hid_low.at[own_slot], hid_low.at[own_slot], z_mate),
         "grad_z": lambda: small("grad_z", grad_part, grad_z, z_mate),
         "low_core": lambda: small(
             "low_core", grad_low.at[pl.ds(row * 4, 4)], grad_low.at[pl.ds(row * 4, 4)], core_mate),
@@ -252,9 +256,10 @@
     for way in (1, 2, 3):
         def along(way=way):
             to_x, to_y = neighbour(0, way), neighbour(1, way)
-            block, plane = pl.ds(x * 8 + y * 2, 2), pl.ds(x * 8, 8)
+            block = pl.ds(y * 2, 2)
             sends[f"hid_y{way}"] = lambda: small(f"hid_y{way}", hid_low.at[block], hid_low.at[block], to_y)
-            sends[f"hid_x{way}"] = lambda: small(f"hid_x{way}", hid_low.at[plane], hid_low.at[plane], to_x)
+            sends[f"hid_x{way}"] = lambda: small(
+                f"hid_x{way}", hid_low.at[own_slot], hid_low.at[own_slot], to_x)
             sends[f"grad_x{way}"] = lambda: small(
                 f"grad_x{way}", grad_sum.at[(x + way) % 4], grad_x.at[x], to_x)
             sends[f"grad_y{way}"] = lambda: small(f"grad_y{way}", grad_y.at[y], grad_y.at[y], to_y)
@@ -327,25 +332,26 @@
 
     def hid_1():
         come("hid_far")
-        hid_low[col] = ((hid_half[...] + hid_far[...]) * INV_WIDTH).astype(jnp.bfloat16)
-        go("hid_z")
-
-    def hid_2():
-        come("hid_z")
-        go(*trio("hid_y"))
-
-    def hid_3():
-        come(*trio("hid_y"))
 
         @pl.when(x == row)
         def _():
+            hid_low[own_slot] = ((hid_half[...] + hid_far[...]) * INV_WIDTH).astype(jnp.bfloat16)
             go(*trio("hid_x"))
 
-    def hid_4():
+    def hid_2():
         for way in (1, 2, 3):
             @pl.when((x - way + 4) % 4 == row)
             def _():
                 sends[f"hid_x{way}"]().wait_recv()
+
+        go("hid_z")
+
+    def hid_3():
+        come("hid_z")
+        go(*trio("hid_y"))
+
+    def hid_4():
+        come(*trio("hid_y"))
 
     def grad_0():
         up_load.wait()
@@ -407,7 +413,7 @@
     def up_0():
         def wide(block, carry):
             start = pl.multiple_of(block * SHARD, SHARD)
-            hid_wide[pl.ds(start, SHARD), :] = widen(hid_low[row * 8 + block], row * 8 * SHARD + start)
+            hid_wide[pl.ds(start, SHARD), :] = widen(hid_low[block], row * 8 * SHARD + start)
             return carry
 
         lax.fori_loop(0, 8, wide, 0)
@@ -446,8 +452,8 @@
         lax.fori_loop(0, 8, adapter, 0)
 
     ahead = {0: [hid_0], 2: [hid_1, grad_1], 4: [hid_2, grad_2], 6: [hid_3, grad_3], 8: [hid_4, grad_4],
-             9: [up_1, grad_5], 11: [up_2]}
-    after = {7: [], 8: [up_0], 9: [grad_6], 10: [adapter_term], 11: [grad_7], 12: [up_3]}
+             9: [grad_5], 10: [up_1], 12: [up_2]}
+    after = {7: [], 8: [up_0], 9: [grad_6, adapter_term], 10: [grad_7], 13: [up_3]}
     grad_0()
     go("grad_z")
 
@@ -555,10 +561,12 @@
                 if step == SWAP_USED:
                     for kind in (0, 1):
                         swap(kind, 1).wait_recv()
+                if step + 2 < COUNT:
+                    send(step + 2)
                 for work in ahead.get(TURN[step], ()):
                     work()
-                if step + 2 < COUNT:
-                    send(step + 2)
+                if step >= 2:
+                    sent(step - 2)
                 if step == SWAP_SENT:
                     for kind in (0, 1):
                         swap(kind, 0).start()
@@ -585,15 +593,20 @@
         @pl.when(group >= CATCH_UP)
         def _():
             def earlier(number, carry):
-                add_down(*group_rows(group_places((group - CATCH_UP) * CATCH_EACH + number)))
+                before = (group - CATCH_UP - 1) * CATCH_EACH + 1 + number
+
+                @pl.when((before >= 0) & (before < CATCH_UP))
+                def _():
+                    add_down(*group_rows(group_places(before)))
+
                 return carry
 
             lax.fori_loop(0, CATCH_EACH, earlier, 0)
 
-        @pl.when(group >= FINISH)
+        @pl.when((group >= FINISH) & (group < FINISH + FINISHED // FINISH_EACH))
         def _():
-            finish(group - FINISH_LAG)
-            finish(group - FINISH)
+            for number in range(FINISH_EACH):
+                finish((group - FINISH) * FINISH_EACH + number)
 
         return carry
 
@@ -604,12 +617,6 @@
     add_down(*group_rows(extra_places))
     extra_sum(1)
 
-    def rest(group, carry):
-        add_down(*group_rows(group_places(group)))
-        return carry
-
-    lax.fori_loop((GROUPS - CATCH_UP) * CATCH_EACH, CATCH_UP, rest, 0)
-
     def moved_down(slot, carry):
         trial = keeper_ref[slot]
         new_down_ref[slot] = down_v[trial] - rate_ref[trial] * (down_sum[trial] * INV_WIDTH)
@@ -621,10 +628,10 @@
         finish(group)
         return carry
 
-    lax.fori_loop(GROUPS - FINISH_LAG, GROUPS + 1, last, 0)
-
-    for step in range(COUNT):
-        every(step, lambda *what: sending(*what).wait_send())
+    lax.fori_loop(FINISHED, GROUPS, last, 0)
+
+    for step in range(COUNT - 3, COUNT):
+        sent(step)
     for kind in (0, 1):
         swap(kind, 0).wait_send()
     for kind in (0, 1):
@@ -642,11 +649,13 @@
         core_copy(number).wait_send()
         return carry
 
+    lax.fori_loop(0, SENT, drain, 0)
+    finish(GROUPS)
+
     def drain_far(number, carry):
         far_copy(number).wait_send()
         return carry
 
-    lax.fori_loop(0, SENT, drain, 0)
     lax.fori_loop(0, 16, drain_far, 0)
 
 
@@ -710,7 +719,7 @@
             pltpu.VMEM((RANK, SHARD), f32),
             pltpu.VMEM((RANK, SHARD), f32),
             pltpu.VMEM((RANK, SHARD), f32),
-            pltpu.VMEM((32, RANK, SHARD), bf16),
+            pltpu.VMEM((8, RANK, SHARD), bf16),
             pltpu.VMEM((4, RANK, 256), f32),
             pltpu.VMEM((4, RANK, 256), f32),
             pltpu.VMEM((4, RANK, 256), f32),

time: 107 us -> 105 us (0.981); the launches traced: 106 us -> 105 us
  no operation moved by 1% of the time
where the time goes in v5:
time: 105 us
  Pallas kernels  105 us (100%)
    pallas_call x1, Pallas kernels, per_device(): pl.pallas_call(whole_kernel, name='adapter_sweep', out_shape=(pltpu.VMEM(...  102 us
    pallas_call x1, Pallas kernels, per_device(): pl.pallas_call(write_out, name='write_out', out_shape=tuple((jax.ShapeDty...  2.24 us

profile of v5, /device:TPU:4, one launch (start us, length us, event | category | flops | bytes accessed | tf_op | source)
XLA Modules:
  0.0 105.2 jit_solution(11554704965368810895)
XLA Ops:
  0.6 102.3 %adapter_sweep.1 = (bf16[1024,896]{1,0:T(8,128)(2,1)S(1)}, f32[16,16,2048]{2,1,0:T(8,128)S(1)}, f32[16,16,896]{2,1,0:T(8,128)S(1)}) custom-call(bf16[128,2048]{1,0:T(8,128)(2,1)} %x_ref.1, bf16[2048,896]{1,0:T(8,128)(2,1)} %w_ref.1, f32[16,16,2048]{2,1,0:T(8,128)} %down_ref.1, f32[16,16,896]{2,1,0:T(8,128)} %up_ref.1, f32[16]{0:T(128)} %rate_ref.1, ...), custom_call_target="tpu_custom_call" | custom-call | flops 22000001024 | bytes 20971520 | tf_op jit(solution)/shard_map/adapter_sweep/pallas_call | solution.py:690
  102.9 2.2 %write_out.1 = (bf16[1024,896]{1,0:T(8,128)(2,1)}, f32[16,16,2048]{2,1,0:T(8,128)}, f32[16,16,896]{2,1,0:T(8,128)}) custom-call(bf16[1024,896]{1,0:T(8,128)(2,1)S(1)} %get-tuple-element.6.refs_0_, f32[16,16,2048]{2,1,0:T(8,128)S(1)} %get-tuple-element.7.refs_1_, f32[16,16,896]{2,1,0:T(8,128)S(1)} %get-tuple-element.8.refs_2_), custom_call_target="tpu_custom_call" | custom-call | tf_op jit(solution)/shard_map/write_out/pallas_call | solution.py:757

commit v6 on v5

--- a/solution.py
+++ b/solution.py
@@ -60,6 +60,21 @@
 TURN = [step + (step >= Z_GROUP) for step in range(COUNT)]
 
 
+def step_of(axis, item):
+    return [item in step for step in STEPS[axis]].index(True)
+
+
+def needed(axis, item):
+    name, zz = item[0], item[-1]
+    if name in ("RF", "RL"):
+        return step_of(axis, ("F" if name == "RF" else "L",) + item[1:])
+    if name == "F" or item[1] == 0:
+        return SWAP_USED if (name, zz) == ("F", 1) else Z_GROUP - 1 if zz else -1
+    if zz:
+        return SWAP_USED if item[1] == 1 else step_of(1 - axis, ("F", 1))
+    return step_of(1 - axis, ("RF" if item[1] == 2 else "F", 0))
+
+
 def offsets(kind, first, last, zz):
     return (first, last, zz, 0) if kind == 0 else (last, first, zz, 1)
 
@@ -109,7 +124,7 @@
     + [f"low_x{k}" for k in (1, 2, 3)] + ["low_core", "low_far", "up_core", "up_far", "up_share"]
 )
 FINISH, FINISH_EACH, FINISHED = 11, 3, 9
-CATCH_UP, CATCH_EACH = 10, 3
+CATCH_UP, CATCH_EACH = 10, 2
 
 
 def select(index, values):
@@ -210,8 +225,12 @@
                 for way in (0, 1):
                     action(axis, way, item)
 
-    def send(step):
-        every(step, lambda *what: sending(*what).start())
+    def send(step, early=None):
+        def start(axis, way, item):
+            if early is None or early == (needed(axis, item) < step - 2):
+                sending(axis, way, item).start()
+
+        every(step, start)
 
     def sent(step):
         every(step, lambda *what: sending(*what).wait_send())
@@ -554,6 +573,8 @@
         for step in range(COUNT - 1):
             @pl.when(group == TURN[step])
             def _():
+                if step + 2 < COUNT:
+                    send(step + 2, early=True)
                 arrive(step)
                 if step == Z_GROUP - 1:
                     for kind in (0, 1):
@@ -562,7 +583,7 @@
                     for kind in (0, 1):
                         swap(kind, 1).wait_recv()
                 if step + 2 < COUNT:
-                    send(step + 2)
+                    send(step + 2, early=False)
                 for work in ahead.get(TURN[step], ()):
                     work()
                 if step >= 2:
@@ -595,7 +616,7 @@
             def earlier(number, carry):
                 before = (group - CATCH_UP - 1) * CATCH_EACH + 1 + number
 
-                @pl.when((before >= 0) & (before < CATCH_UP))
+                @pl.when((before >= 0) & (before < 7))
                 def _():
                     add_down(*group_rows(group_places(before)))
 
@@ -616,6 +637,12 @@
     extra_product(1)
     add_down(*group_rows(extra_places))
     extra_sum(1)
+
+    def rest(group, carry):
+        add_down(*group_rows(group_places(group)))
+        return carry
+
+    lax.fori_loop(7, CATCH_UP, rest, 0)
 
     def moved_down(slot, carry):
         trial = keeper_ref[slot]

time: 105 us -> 105 us (level)
  no operation moved by 1% of the time
where the time goes in v6:
time: 105 us
  Pallas kernels  104 us (99%)
    pallas_call x1, Pallas kernels, per_device(): pl.pallas_call(whole_kernel, name='adapter_sweep', out_shape=(pltpu.VMEM(...  102 us
    pallas_call x1, Pallas kernels, per_device(): pl.pallas_call(write_out, name='write_out', out_shape=tuple((jax.ShapeDty...  2.24 us

profile of v6, /device:TPU:4, one launch (start us, length us, event | category | flops | bytes accessed | tf_op | source)
XLA Modules:
  0.0 104.9 jit_solution(14102585976703258386)
XLA Ops:
  0.6 102.0 %adapter_sweep.1 = (bf16[1024,896]{1,0:T(8,128)(2,1)S(1)}, f32[16,16,2048]{2,1,0:T(8,128)S(1)}, f32[16,16,896]{2,1,0:T(8,128)S(1)}) custom-call(bf16[128,2048]{1,0:T(8,128)(2,1)} %x_ref.1, bf16[2048,896]{1,0:T(8,128)(2,1)} %w_ref.1, f32[16,16,2048]{2,1,0:T(8,128)} %down_ref.1, f32[16,16,896]{2,1,0:T(8,128)} %up_ref.1, f32[16]{0:T(128)} %rate_ref.1, ...), custom_call_target="tpu_custom_call" | custom-call | flops 22000001024 | bytes 20971520 | tf_op jit(solution)/shard_map/adapter_sweep/pallas_call | solution.py:717
  102.6 2.2 %write_out.1 = (bf16[1024,896]{1,0:T(8,128)(2,1)}, f32[16,16,2048]{2,1,0:T(8,128)}, f32[16,16,896]{2,1,0:T(8,128)}) custom-call(bf16[1024,896]{1,0:T(8,128)(2,1)S(1)} %get-tuple-element.6.refs_0_, f32[16,16,2048]{2,1,0:T(8,128)S(1)} %get-tuple-element.7.refs_1_, f32[16,16,896]{2,1,0:T(8,128)S(1)} %get-tuple-element.8.refs_2_), custom_call_target="tpu_custom_call" | custom-call | tf_op jit(solution)/shard_map/write_out/pallas_call | solution.py:784

commit v7 on v5

--- a/solution.py
+++ b/solution.py
@@ -612,17 +612,17 @@
 
     lax.fori_loop(0, GROUPS, body, 0)
 
-    arrive(COUNT - 1)
-    extra_product(1)
-    add_down(*group_rows(extra_places))
-    extra_sum(1)
-
     def moved_down(slot, carry):
         trial = keeper_ref[slot]
         new_down_ref[slot] = down_v[trial] - rate_ref[trial] * (down_sum[trial] * INV_WIDTH)
         return carry
 
+    arrive(COUNT - 1)
+    extra_product(1)
+    add_down(*group_rows(extra_places))
     lax.fori_loop(0, TRIALS, moved_down, 0)
+    extra_sum(1)
+
 
     def last(group, carry):
         finish(group)

time: 105 us -> 105 us (level)
  no operation moved by 1% of the time
where the time goes in v7:
time: 105 us
  Pallas kernels  105 us (100%)
    pallas_call x1, Pallas kernels, per_device(): pl.pallas_call(whole_kernel, name='adapter_sweep', out_shape=(pltpu.VMEM(...  102 us
    pallas_call x1, Pallas kernels, per_device(): pl.pallas_call(write_out, name='write_out', out_shape=tuple((jax.ShapeDty...  2.24 us

profile of v7, /device:TPU:4, one launch (start us, length us, event | category | flops | bytes accessed | tf_op | source)
XLA Modules:
  0.0 105.2 jit_solution(10004922495517978297)
XLA Ops:
  0.6 102.3 %adapter_sweep.1 = (bf16[1024,896]{1,0:T(8,128)(2,1)S(1)}, f32[16,16,2048]{2,1,0:T(8,128)S(1)}, f32[16,16,896]{2,1,0:T(8,128)S(1)}) custom-call(bf16[128,2048]{1,0:T(8,128)(2,1)} %x_ref.1, bf16[2048,896]{1,0:T(8,128)(2,1)} %w_ref.1, f32[16,16,2048]{2,1,0:T(8,128)} %down_ref.1, f32[16,16,896]{2,1,0:T(8,128)} %up_ref.1, f32[16]{0:T(128)} %rate_ref.1, ...), custom_call_target="tpu_custom_call" | custom-call | flops 22000001024 | bytes 20971520 | tf_op jit(solution)/shard_map/adapter_sweep/pallas_call | solution.py:690
  102.9 2.2 %write_out.1 = (bf16[1024,896]{1,0:T(8,128)(2,1)}, f32[16,16,2048]{2,1,0:T(8,128)}, f32[16,16,896]{2,1,0:T(8,128)}) custom-call(bf16[1024,896]{1,0:T(8,128)(2,1)S(1)} %get-tuple-element.6.refs_0_, f32[16,16,2048]{2,1,0:T(8,128)S(1)} %get-tuple-element.7.refs_1_, f32[16,16,896]{2,1,0:T(8,128)S(1)} %get-tuple-element.8.refs_2_), custom_call_target="tpu_custom_call" | custom-call | tf_op jit(solution)/shard_map/write_out/pallas_call | solution.py:757
